TPU v7x, 256 devices: a whole 4x4x8 slice. The times are simulated.
256 devices in a mesh: row: 8 (over x_hi, y), col: 8 (over z), scene: 4 (over x_lo, core).
Axes of the slice: x: 4 (x_hi: 2, x_lo: 2; x = x_hi * 2 + x_lo), y: 4, z: 8, core: 2. Of those that a mesh axis runs over, the one named last changes fastest.
Arguments:
- features: bfloat16 [8, 112, 112, 384], P('scene', 'row', 'col'), may hold values from -6 to 6
- grad_out: bfloat16 [8, 112, 112, 384], P('scene', 'row', 'col'), may hold values from -6 to 6
- norm_gain: float32 [384], replicated, may hold values from 0.1 to 1.9
- norm_shift: float32 [384], replicated, may hold values from -3 to 3
- qkv_weight: bfloat16 [384, 1152], replicated, may hold values from -0.3125 to 0.3125
- qkv_bias: float32 [1152], replicated, may hold values from -3 to 3
- proj_weight: bfloat16 [384, 384], replicated, may hold values from -0.3125 to 0.3125
- bias_table: float32 [169, 12], replicated, may hold values from -8 to 320
Outputs:
- grad_x: bfloat16 [8, 112, 112, 384], P('scene', 'row', 'col')
- grad_gain: float32 [384], replicated
- grad_shift: float32 [384], replicated
- grad_wqkv: float32 [384, 1152], replicated
- grad_bqkv: float32 [1152], replicated
- grad_wproj: float32 [384, 384], replicated
- grad_bproj: float32 [384], replicated
- grad_table: float32 [169, 12], replicated
All inputs are finite; a program needn't handle non-finite values.
Results may differ from a plain program's by a relative error of at most 0.025.
Values may be sent and summed in bfloat16 or wider, within the bound.
A program may use at most 64 MiB of HBM per device.

v0:
```python
import math

import jax
import jax.numpy as jnp
from jax import lax
from jax.sharding import PartitionSpec as P

WIN = 7
SHIFT = 3


NORM_EPS = 1e-05
MASKED_SCORE = -1e30


def from_behind(value, axis, by):
    size = lax.axis_size(axis)
    return lax.ppermute(value, axis, [(i, (i + by) % size) for i in range(size)])


def layer_norm(tokens, norm_gain, norm_shift):
    values = tokens.astype(jnp.float32)
    average = jnp.mean(values, axis=-1, keepdims=True)
    centered = values - average
    variance = jnp.mean(centered * centered, axis=-1, keepdims=True)
    return (centered * lax.rsqrt(variance + NORM_EPS) * norm_gain + norm_shift).astype(jnp.bfloat16)


def to_windows(grid, side):
    scene_count, row_count, col_count, chan_count = grid.shape
    grid = grid.reshape(scene_count, row_count // side, side, col_count // side, side, chan_count)
    grid = grid.transpose(0, 1, 3, 2, 4, 5)
    return grid.reshape(-1, side * side, chan_count)


def from_windows(windows, side, scene_count, row_count, col_count):
    chan_count = windows.shape[-1]
    grid = windows.reshape(
        scene_count, row_count // side, col_count // side, side, side, chan_count
    )
    grid = grid.transpose(0, 1, 3, 2, 4, 5)
    return grid.reshape(scene_count, row_count, col_count, chan_count)


def band_of(places, total):
    return (places >= total - WIN).astype(jnp.int32) + (places >= total - SHIFT).astype(jnp.int32)


def relative_bias(bias_table, side):
    cell_count = side * side
    places = jnp.arange(cell_count, dtype=jnp.int32)
    row_of = places // side
    col_of = places % side
    index_grid = (row_of[:, None] - row_of[None, :] + side - 1) * (2 * side - 1) + (
        col_of[:, None] - col_of[None, :] + side - 1
    )
    offsets = jnp.arange(bias_table.shape[0], dtype=jnp.int32)
    one_hot = (index_grid[:, :, None] == offsets[None, None, :]).astype(jnp.float32)
    return jnp.einsum("qkt,th->hqk", one_hot, bias_table, precision=lax.Precision.HIGHEST)


def window_attention(qkv_win, bias_table, region_win, side):
    win_count, cell_count, triple = qkv_win.shape
    heads_count = bias_table.shape[1]
    chan_count = triple // 3
    head_size = chan_count // heads_count
    split_parts = qkv_win.astype(jnp.float32).reshape(
        win_count, cell_count, 3, heads_count, head_size
    )
    queries = split_parts[:, :, 0]
    keys_all = split_parts[:, :, 1]
    values = split_parts[:, :, 2]
    scores = jnp.einsum(
        "bqhd,bkhd->bhqk", queries, keys_all, precision=lax.Precision.HIGHEST
    ) * head_size ** (-0.5)
    scores = scores + relative_bias(bias_table, side)[None]
    same_region = region_win[:, None, :, None] == region_win[:, None, None, :]
    scores = jnp.where(same_region, scores, MASKED_SCORE)
    weights = jax.nn.softmax(scores, axis=-1).astype(jnp.bfloat16)
    mixed_heads = jnp.einsum(
        "bhqk,bkhd->bqhd", weights.astype(jnp.float32), values, precision=lax.Precision.HIGHEST
    )
    return mixed_heads.reshape(win_count, cell_count, chan_count).astype(jnp.bfloat16)


def on_device(
    features, grad_out, norm_gain, norm_shift, qkv_weight, qkv_bias, proj_weight, bias_table
):
    scene_count, row_count, col_count, chan_count = features.shape
    total_rows = row_count * lax.axis_size("row")
    total_cols = col_count * lax.axis_size("col")
    joined = jnp.stack([features, grad_out])
    from_below = from_behind(joined[:, :, :SHIFT], "row", -1)
    joined = jnp.concatenate([joined[:, :, SHIFT:], from_below], axis=2)
    from_right = from_behind(joined[:, :, :, :SHIFT], "col", -1)
    joined = jnp.concatenate([joined[:, :, :, SHIFT:], from_right], axis=3)
    shifted = joined[0]
    upstream = joined[1]
    row_places = lax.axis_index("row") * row_count + jnp.arange(row_count, dtype=jnp.int32)
    col_places = lax.axis_index("col") * col_count + jnp.arange(col_count, dtype=jnp.int32)
    region_tile = (
        3 * band_of(row_places, total_rows)[:, None] + band_of(col_places, total_cols)[None, :]
    )
    region = jnp.broadcast_to(region_tile[None], (scene_count, row_count, col_count))
    flat = shifted.reshape(-1, chan_count)
    normed, norm_back = jax.vjp(layer_norm, flat, norm_gain, norm_shift)
    qkv = (jnp.dot(normed, qkv_weight, preferred_element_type=jnp.float32) + qkv_bias).astype(
        jnp.bfloat16
    )
    qkv_win = to_windows(qkv.reshape(scene_count, row_count, col_count, 3 * chan_count), WIN)
    region_win = to_windows(region[..., None], WIN)[..., 0]

    def attend(qkv_in, table_in):
        return window_attention(qkv_in, table_in, region_win, WIN)

    attn_win, attn_back = jax.vjp(attend, qkv_win, bias_table)
    attended = from_windows(attn_win, WIN, scene_count, row_count, col_count).reshape(
        -1, chan_count
    )
    incoming = upstream.reshape(-1, chan_count)
    grad_wproj = jnp.dot(attended.T, incoming, preferred_element_type=jnp.float32)
    grad_bproj = jnp.sum(incoming.astype(jnp.float32), axis=0)
    grad_attn = jnp.dot(incoming, proj_weight.T, preferred_element_type=jnp.float32).astype(
        jnp.bfloat16
    )
    grad_attn_win = to_windows(
        grad_attn.reshape(scene_count, row_count, col_count, chan_count), WIN
    )
    grad_qkv_win, grad_table = attn_back(grad_attn_win)
    grad_qkv = from_windows(grad_qkv_win, WIN, scene_count, row_count, col_count).reshape(
        -1, 3 * chan_count
    )
    grad_wqkv = jnp.dot(normed.T, grad_qkv, preferred_element_type=jnp.float32)
    grad_bqkv = jnp.sum(grad_qkv.astype(jnp.float32), axis=0)
    grad_normed = jnp.dot(grad_qkv, qkv_weight.T, preferred_element_type=jnp.float32).astype(
        jnp.bfloat16
    )
    grad_flat, grad_gain, grad_shift = norm_back(grad_normed)
    total_gain, total_shift, total_wqkv, total_bqkv, total_wproj, total_bproj, total_table = (
        lax.psum(
            (grad_gain, grad_shift, grad_wqkv, grad_bqkv, grad_wproj, grad_bproj, grad_table),
            ("row", "col", "scene"),
        )
    )
    grad_shifted = grad_flat.reshape(scene_count, row_count, col_count, chan_count)
    from_left = from_behind(grad_shifted[:, :, col_count - SHIFT :], "col", 1)
    grad_cols = jnp.concatenate([from_left, grad_shifted[:, :, : col_count - SHIFT]], axis=2)
    from_above = from_behind(grad_cols[:, row_count - SHIFT :], "row", 1)
    grad_local = jnp.concatenate([from_above, grad_cols[:, : row_count - SHIFT]], axis=1)
    grad_x = (grad_out.astype(jnp.float32) + grad_local.astype(jnp.float32)).astype(jnp.bfloat16)
    scale = 1.0 / math.sqrt(
        scene_count
        * row_count
        * col_count
        * lax.axis_size("row")
        * lax.axis_size("col")
        * lax.axis_size("scene")
    )
    return (
        grad_x,
        total_gain * scale,
        total_shift * scale,
        total_wqkv * scale,
        total_bqkv * scale,
        total_wproj * scale,
        total_bproj * scale,
        total_table * scale,
    )


def solution(mesh):
    return jax.shard_map(
        on_device,
        mesh=mesh,
        in_specs=(
            P("scene", "row", "col", None),
            P("scene", "row", "col", None),
            P(),
            P(),
            P(),
            P(),
            P(),
            P(),
        ),
        out_specs=(P("scene", "row", "col", None), P(), P(), P(), P(), P(), P(), P()),
        check_vma=False,
    )
```

profile of v0, /device:TPU:1, one launch (start us, length us, event | category | flops | bytes accessed | tf_op | source)
XLA Modules:
  0.0 461.0 jit_solution(14036058176576960114)
XLA Ops:
  7.2 1.1 pad_maximum_fusion.3
  8.4 6.1 %collective-permute-start = (bf16[2,2,3,14,384]{4,1,3,2,0:T(2,128)(2,1)S(1)}, bf16[2,2,3,14,384]{4,1,3,2,0:T(2,128)(2,1)S(1)}, u32[]{:S(2)}, u32[]{:S(2)}) collective-permute-start(bf16[2,2,3,14,384]{4,1,3,2,0:T(2,128)(2,1)S(1)} %pad_maximum_fusion.3), channel_id=1, source_target_pairs={{0,224},{32,0},{64,32},{96,64},{128,96},{160,128},{192,160},{224,1... | collective-permute-start | bytes 387080 | tf_op jit(solution)/shard_map/ppermute | solution.py:18
  15.3 2.7 fusion.30
  18.0 1.8 fusion.40
  20.0 6.1 %collective-permute-start.1 = (bf16[2,2,14,3,384]{4,1,3,2,0:T(2,128)(2,1)S(1)}, bf16[2,2,14,3,384]{4,1,3,2,0:T(2,128)(2,1)S(1)}, u32[]{:S(2)}, u32[]{:S(2)}) collective-permute-start(bf16[2,2,14,3,384]{4,1,3,2,0:T(2,128)(2,1)S(1)} %pad_maximum_fusion.2), channel_id=1, source_target_pairs={{0,28},{4,0},{8,4},{12,8},{16,12},{20,16},{24,20},{28,24},{1,29},{... | collective-permute-start | bytes 387080 | tf_op jit(solution)/shard_map/ppermute | solution.py:18
  26.1 0.7 broadcast_compare_fusion
  28.0 1.4 convert_reduce_fusion.1
  29.7 0.6 multiply_reduce_fusion.2
  30.5 0.7 fusion.55
  32.2 1.4 convolution_convert_fusion.3
  33.7 1.0 copy.50
  34.8 0.8 copy-done.7
  35.6 1.7 fusion.1
  37.2 1.4 reshape_reshape.13
  38.6 1.6 copy.54
  40.3 2.5 reshape.268
  42.8 2.3 copy.58
  45.1 6.9 %reshape.269 = bf16[8,49,3,12,32]{4,3,2,0,1:T(8,128)(2,1)} reshape(bf16[2,2,2,7,7,1152]{5,2,1,0,4,3:T(2,128)(2,1)} %copy.54) | data formatting | bytes 1806336 | tf_op jit(solution)/shard_map/jvp()/reshape | solution.py:67
  52.0 5.8 %fusion.61 = (bf16[8,49,1,12,32]{4,3,2,0,1:T(8,128)(2,1)}, bf16[8,49,1,12,32]{4,3,2,0,1:T(8,128)(2,1)}, bf16[8,49,1,12,32]{4,3,2,0,1:T(8,128)(2,1)S(1)}) fusion(bf16[8,49,3,12,32]{4,3,2,0,1:T(8,128)(2,1)} %reshape.269), kind=kLoop, calls=%fused_computation.115 | loop fusion | bytes 1806336 | tf_op jit(solution)/shard_map/jvp()/slice | solution.py:72
  57.7 3.3 copy.78
  61.1 3.3 copy.77
  64.4 2.4 copy.76
  66.8 2.3 fusion.35
  69.1 1.1 fusion.62
  70.3 1.4 fusion.28
  71.7 1.0 fusion.8
  72.7 0.9 fusion.57
  73.8 3.2 fusion.17
  77.1 3.9 fusion.14
  81.0 2.0 convolution_bitcast_fusion
  83.6 0.8 convert_element_type.135
  84.7 1.1 fusion.31
  85.8 4.1 copy.68
  89.9 1.0 convert_element_type.139
  91.1 1.2 fusion.64
  92.3 3.0 add_convert_fusion
  95.3 9.0 %copy.64 = bf16[8,49,3,12,32]{4,3,2,0,1:T(8,128)(2,1)} copy(bf16[8,49,3,12,32]{1,4,3,0,2:T(8,128)(2,1)S(1)} %add_convert_fusion) | data formatting | bytes 1806336 | tf_op jit(solution)/shard_map/transpose(jvp())/convert_element_type | solution.py:67
  104.4 6.4 %convert_element_type.128 = bf16[2,2,2,7,7,1152]{5,2,1,0,4,3:T(2,128)(2,1)S(1)} reshape(bf16[8,49,3,12,32]{4,3,2,0,1:T(8,128)(2,1)} %copy.64) | data formatting | bytes 1806336 | tf_op jit(solution)/shard_map/transpose(jvp())/convert_element_type | solution.py:67
  110.8 0.8 convert_reduce_fusion
  112.1 0.9 multiply_reduce_fusion
  113.3 75.9 %all-reduce.3 = (f32[384]{0:T(512)S(1)}, f32[384]{0:T(512)S(1)}, f32[1152]{0:T(1024)S(1)}, f32[384]{0:T(512)S(1)}, f32[169,12]{0,1:T(8,128)S(1)}) all-reduce(f32[384]{0:T(512)S(1)} %get-tuple-element.24, f32[384]{0:T(512)S(1)} %get-tuple-element.26, ...), channel_id=1, replica_groups=mesh['row'=8,'col'=8,'scene'=4] {'row','col','scene'}, use_global_device_ids=true, to_apply=%region_8.9 | all-reduce | flops 4332 | bytes 34656 | tf_op jit(solution)/shard_map/psum | solution.py:140
  190.2 3.2 fusion.63
  195.3 1.0 collective-permute-start.3
  196.9 5.3 %collective-permute-done.3 = bf16[2,3,14,384]{3,2,1,0:T(8,128)(2,1)S(1)} collective-permute-done((bf16[2,3,14,384]{3,2,1,0:T(8,128)(2,1)S(1)}, bf16[2,3,14,384]{3,2,1,0:T(8,128)(2,1)S(1)}, u32[]{:S(2)}, u32[]{:S(2)}) %collective-permute-start.3) | collective-permute-done | bytes 64544 | tf_op jit(solution)/shard_map/ppermute | solution.py:18
  202.3 0.9 copy.71
  203.3 246.8 %all-reduce.7.cloned.1.call-done = (f32[384,1152]{1,0:T(8,128)}, f32[384,384]{1,0:T(8,128)}) async-done(((f32[384,1152]{1,0:T(8,128)}, f32[384,384]{1,0:T(8,128)}), (f32[384,1152]{1,0:T(8,128)}, f32[384,384]{1,0:T(8,128)})) %all-reduce.7.cloned.1.call-update) | async-done | bytes 2359312 | tf_op jit(solution)/shard_map/psum | solution.py:140
  450.1 2.9 broadcast_multiply_fusion
  453.0 0.9 broadcast_multiply_fusion.1
  (99 shorter events, 9.5 us)
Async XLA Ops:
  7.2 28.4 %copy-start = (bf16[384,1152]{1,0:T(8,128)(2,1)S(1)}, bf16[384,1152]{1,0:T(8,128)(2,1)}, u32[]{:S(2)}) copy-start(bf16[384,1152]{1,0:T(8,128)(2,1)} %param.12) | copy-start | bytes 2654212
  7.2 442.9 %all-reduce.7.cloned.1.call-start = ((), (), s32[]{:S(2)}) async-start(), calls=%async_computation | async-start | bytes 4718592 | tf_op jit(solution)/shard_map/psum | solution.py:140
  8.4 11.4 %collective-permute-start = (bf16[2,2,3,14,384]{4,1,3,2,0:T(2,128)(2,1)S(1)}, bf16[2,2,3,14,384]{4,1,3,2,0:T(2,128)(2,1)S(1)}, u32[]{:S(2)}, u32[]{:S(2)}) collective-permute-start(bf16[2,2,3,14,384]{4,1,3,2,0:T(2,128)(2,1)S(1)} %pad_maximum_fusion.3), channel_id=1, source_target_pairs={{0,224},{32,0},{64,32},{96,64},{128,96},{160,128},{192,160},{224,1... | collective-permute-start | bytes 387080 | tf_op jit(solution)/shard_map/ppermute | solution.py:18
  14.7 0.6 copy-start.12
  20.0 8.0 %collective-permute-start.1 = (bf16[2,2,14,3,384]{4,1,3,2,0:T(2,128)(2,1)S(1)}, bf16[2,2,14,3,384]{4,1,3,2,0:T(2,128)(2,1)S(1)}, u32[]{:S(2)}, u32[]{:S(2)}) collective-permute-start(bf16[2,2,14,3,384]{4,1,3,2,0:T(2,128)(2,1)S(1)} %pad_maximum_fusion.2), channel_id=1, source_target_pairs={{0,28},{4,0},{8,4},{12,8},{16,12},{20,16},{24,20},{28,24},{1,29},{... | collective-permute-start | bytes 387080 | tf_op jit(solution)/shard_map/ppermute | solution.py:18
  30.4 5.2 %copy-start.17 = (f32[384]{0:T(512)S(1)}, f32[384]{0:T(512)}, u32[]{:S(2)}) copy-start(f32[384]{0:T(512)} %param.10) | copy-start | bytes 4612
  30.4 5.2 %copy-start.23 = (f32[384]{0:T(512)S(1)}, f32[384]{0:T(512)}, u32[]{:S(2)}) copy-start(f32[384]{0:T(512)} %param.11) | copy-start | bytes 4612
  30.4 5.2 %copy-start.25 = (f32[1152]{0:T(1024)S(1)}, f32[1152]{0:T(1024)}, u32[]{:S(2)}) copy-start(f32[1152]{0:T(1024)} %param.13) | copy-start | bytes 13828
  30.5 6.7 %copy-start.19 = (f32[392]{0:T(512)}, f32[392]{0:T(512)S(1)}, u32[]{:S(2)}) copy-start(f32[392]{0:T(512)S(1)} %div.59) | copy-start | bytes 4708
  31.5 0.6 copy-start.14
  32.1 5.2 %copy-start.21 = (f32[392]{0:T(512)}, f32[392]{0:T(512)S(1)}, u32[]{:S(2)}) copy-start(f32[392]{0:T(512)S(1)} %rsqrt.13) | copy-start | bytes 4708
  34.7 0.8 copy-start.7
  66.8 2.3 copy-start.10
  69.1 1.1 copy-start.5
  70.3 1.4 copy-start.2
  72.7 1.1 copy-start.3
  73.8 3.2 copy-start.4
  81.0 2.0 copy-start.11
  81.0 2.0 copy-start.18
  81.0 2.0 copy-start.24
  83.0 1.7 copy-start.13
  110.8 1.3 copy-start.8
  110.8 1.3 copy-start.20
  110.8 1.3 copy-start.22
  111.7 1.2 copy-start.15
  112.1 77.8 %copy-start.1 = (bf16[392,1152]{1,0:T(8,128)(2,1)}, bf16[392,1152]{1,0:T(8,128)(2,1)S(1)}, u32[]{:S(2)}) copy-start(bf16[392,1152]{1,0:T(8,128)(2,1)S(1)} %reshape_reshape.14) | copy-start | bytes 2709508
  112.1 1.2 copy-start.16
  190.1 12.0 %copy-start.6 = (bf16[2,14,14,384]{3,0,2,1:T(2,128)(2,1)S(1)}, bf16[2,14,14,384]{3,0,2,1:T(2,128)(2,1)}, u32[]{:S(2)}) copy-start(bf16[2,14,14,384]{3,0,2,1:T(2,128)(2,1)} %param.9) | copy-start | bytes 903172
  190.2 5.1 %collective-permute-start.2 = (bf16[2,14,3,384]{3,2,1,0:T(4,128)(2,1)S(1)}, bf16[2,14,3,384]{3,2,1,0:T(4,128)(2,1)S(1)}, u32[]{:S(2)}, u32[]{:S(2)}) collective-permute-start(bf16[2,14,3,384]{3,2,1,0:T(4,128)(2,1)S(1)} %slice.61), channel_id=1, source_target_pairs={{0,4},{4,8},{8,12},{12,16},{16,20},{20,24},{24,28},{28,0},{1,5},{5... | collective-permute-start | bytes 193544 | tf_op jit(solution)/shard_map/ppermute | solution.py:18
  195.3 6.9 %collective-permute-start.3 = (bf16[2,3,14,384]{3,2,1,0:T(8,128)(2,1)S(1)}, bf16[2,3,14,384]{3,2,1,0:T(8,128)(2,1)S(1)}, u32[]{:S(2)}, u32[]{:S(2)}) collective-permute-start(bf16[2,3,14,384]{3,2,1,0:T(8,128)(2,1)S(1)} %pad_maximum_fusion.4), channel_id=1, source_target_pairs={{0,32},{32,64},{64,96},{96,128},{128,160},{160,192},{192,224},{224... | collective-permute-start | bytes 193544 | tf_op jit(solution)/shard_map/ppermute | solution.py:18
  450.1 2.9 copy-start.9
Sparse Core Ops, SparseCore 0:
  193.6 256.4 all-reduce.6
where the time goes:
time: 466 us; the launch traced here: 461 us
  waiting for transfers between devices  252 us (54%)
  blocking collectives  75.9 us (16%)
  local copies, waits for them, and re-layouts  57.5 us (12%)
  matrix products  25.9 us (6%)
  other arithmetic  21 us (5%)
  between operations  14.8 us (3%)
  starting transfers between devices  13.4 us (3%)
    psum x1, waiting for transfers between devices, on_device(): lax.psum((grad_gain, grad_shift, grad_wqkv, grad_bqkv, grad_wproj, grad_b...  247 us
    psum x1, blocking collectives, on_device(): lax.psum((grad_gain, grad_shift, grad_wqkv, grad_bqkv, grad_wproj, grad_b...  75.9 us
    convert_element_type x2, local copies, waits for them, and re-layouts, window_attention(): qkv_win.astype(jnp.float32)  15.4 us
    ppermute x4, starting transfers between devices, from_behind(): lax.ppermute(value, axis, [(i, (i + by) % size) for i in range(size)])  13.3 us
    unnamed x56, local copies, waits for them, and re-layouts  12.4 us
    dot_general x3, matrix products, window_attention(): jnp.einsum('bqhd,bkhd->bhqk', queries, keys_all, precision=lax.Precision....  9.43 us
  transfers between devices with their start and end apart: 5, of which 3 were waited for; matrix products, arithmetic and copies ran while one was open for 3% of the time, Pallas kernels for 0%

commit v1 on v0

v1 whole, which is shorter than its diff:
```python
import functools
import math

import jax
import jax.numpy as jnp
import numpy as np
from jax import lax
from jax.experimental import pallas as pl
from jax.experimental.pallas import tpu as pltpu
from jax.sharding import PartitionSpec as P
MESH = pl.DeviceIdType.MESH
f32, bf16 = jnp.float32, jnp.bfloat16
CH = 10

def place():
    row, z, scene = lax.axis_index("row"), lax.axis_index("col"), lax.axis_index("scene")
    x = (row // 4) * 2 + scene // 2
    return x, row % 4, z, scene % 2

def at(x, y, z, core):
    return ((x // 2) * 4 + y, z, (x % 2) * 2 + core)

def pack(total):
    big = total[:9].astype(bf16)
    t = total[9, :8] + total[9, 8:]
    hi = t.astype(bf16).astype(f32)
    small = jnp.concatenate([hi, t - hi], axis=0).astype(bf16)
    return big, small

def reduce_kernel(stop, g, h, out, hout, r0, s1, r1, s2, r2, acc,
                  h_s, h_r, p0s, p0r, p1s, p1r, p2s, p2r, p3s, p3r, p4s, p4r, p5s, p5r):
    x, y, z, core = place()
    me = x * 4 + y
    row, scene = lax.axis_index("row"), lax.axis_index("scene")
    def plane(k):
        return lax.rem(x + k // 4, 4), lax.rem(y + k % 4, 4)
    bar = pltpu.get_barrier_semaphore()
    def greet(dev):
        pl.semaphore_signal(bar, inc=1, device_id=dev, device_id_type=MESH)
    greet(at(x, y, z, 1 - core))
    for k in range(1, 16):
        px, py = plane(k)
        greet(at(px, py, z, core))
    for k in range(1, 8):
        greet(at(x, y, lax.rem(z + k, 8), core))
    rm, zm = lax.rem(row + 7, 8), lax.rem(z + 7, 8)
    rp, zp = lax.rem(row + 1, 8), lax.rem(z + 1, 8)
    for d in ((rm, z, scene), (row, zm, scene), (rm, zm, scene)):
        greet(d)
    pl.semaphore_wait(bar, 1 + 15 + 7 + 3)

    def rc(src, dst, ss, rs, dev):
        return pltpu.make_async_remote_copy(src_ref=src, dst_ref=dst, send_sem=ss, recv_sem=rs, device_id=dev, device_id_type=MESH)
    sib = at(x, y, z, 1 - core)
    pend = []
    def chunk(k):
        return lax.rem(me // 4 + k // 4, 4) * 4 + lax.rem(me % 4 + k % 4, 4)
    order = list(range(1, 16)) + [0]
    c0 = [None] * 16
    for k in order:
        c = chunk(k)
        c0[k] = rc(g.at[(1 - core) * 16 + c], r0.at[c], p0s.at[k], p0r.at[k], sib)
        c0[k].start()
    hc = []
    for i, (d, lo, n) in enumerate((((rp, z, scene), 0, 80), ((row, zp, scene), 80, 80), ((rp, zp, scene), 160, 32))):
        cp = rc(h.at[pl.ds(lo, n)], hout.at[pl.ds(lo, n)], h_s.at[i], h_r.at[i], d)
        cp.start()
        hc.append(cp)
    c1 = [None] * 16
    for k in order:
        c = chunk(k)
        c0[k].wait_recv()
        total = g[core * 16 + c].astype(f32) + r0[c].astype(f32)
        if k:
            big, small = pack(total)
            s1[c, :9] = big
            s1[c, 9] = small
            if stop >= 1:
                px, py = plane(k)
                c1[k] = rc(s1.at[c], r1.at[k], p1s.at[k], p1r.at[k], at(px, py, z, core))
                c1[k].start()
        else:
            acc[...] = total
    if stop >= 1:
        for k in range(1, 16):
            c1[k].wait_recv()
            acc[...] += r1[k].astype(f32)
    big, small = pack(acc[...])
    for t in range(8):
        s2[t, 0] = big[t]
        s2[t, 1] = big[8]
        s2[t, 2] = small
    c2, c3 = [None] * 8, [None] * 8
    if stop >= 2:
        for k in range(1, 8):
            d = lax.rem(z + k, 8)
            c2[k] = rc(s2.at[d], r2.at[z], p2s.at[k], p2r.at[k], at(x, y, d, core))
            c2[k].start()
        r2[z] = s2[z]
        for k in range(1, 8):
            fr = lax.rem(z + 8 - k, 8)
            rc(s2.at[fr], r2.at[fr], p2s.at[k], p2r.at[k], at(x, y, fr, core)).wait_recv()
        t3 = r2[0].astype(f32)
        for t in range(1, 8):
            t3 += r2[t].astype(f32)
        tt = t3[2, :8] + t3[2, 8:]
        hi = tt.astype(bf16).astype(f32)
        mine = core * 16 + me
        out[mine, z] = t3[0].astype(bf16)
        out[mine, 8] = t3[1].astype(bf16)
        out[mine, 9] = jnp.concatenate([hi, tt - hi], axis=0).astype(bf16)
        for k in range(1, 8):
            d = lax.rem(z + k, 8)
            c3[k] = rc(out.at[mine, z], out.at[mine, z], p3s.at[k], p3r.at[k], at(x, y, d, core))
            c3[k].start()
        for k in range(1, 8):
            fr = lax.rem(z + 8 - k, 8)
            rc(out.at[mine, fr], out.at[mine, fr], p3s.at[k], p3r.at[k], at(x, y, fr, core)).wait_recv()
    c4, c5 = [None] * 16, [None] * 16
    if stop >= 3:
        mine = core * 16 + me
        for k in range(1, 16):
            px, py = plane(k)
            c4[k] = rc(out.at[mine], out.at[mine], p4s.at[k], p4r.at[k], at(px, py, z, core))
            c4[k].start()
        if stop >= 4:
            c5[0] = rc(out.at[mine], out.at[mine], p5s.at[0], p5r.at[0], sib)
            c5[0].start()
        for k in range(1, 16):
            fx, fy = lax.rem(x + 4 - k // 4, 4), lax.rem(y + 4 - k % 4, 4)
            f = core * 16 + fx * 4 + fy
            rc(out.at[f], out.at[f], p4s.at[k], p4r.at[k], at(fx, fy, z, core)).wait_recv()
            if stop >= 4:
                c5[k] = rc(out.at[f], out.at[f], p5s.at[k], p5r.at[k], sib)
                c5[k].start()
        if stop >= 4:
            for k in range(16):
                fx, fy = lax.rem(x + 4 - k // 4, 4), lax.rem(y + 4 - k % 4, 4)
                f = (1 - core) * 16 + fx * 4 + fy
                rc(out.at[f], out.at[f], p5s.at[k], p5r.at[k], sib).wait_recv()
    for cp in hc:
        cp.wait_recv()
    for cp in hc + c0 + c1 + c2 + c3 + c4 + c5:
        if cp is not None:
            cp.wait_send()

def reduce_all(g, h, stop=4):
    V = pl.BlockSpec(memory_space=pltpu.VMEM)
    D = pltpu.SemaphoreType.DMA
    return pl.pallas_call(
        functools.partial(reduce_kernel, stop),
        out_shape=(jax.ShapeDtypeStruct((32, CH, 16, 128), bf16), jax.ShapeDtypeStruct((192, 384), bf16)),
        in_specs=[V, V], out_specs=(V, V),
        scratch_shapes=[
            pltpu.VMEM((16, CH, 16, 128), bf16), pltpu.VMEM((16, CH, 16, 128), bf16), pltpu.VMEM((16, CH, 16, 128), bf16),
            pltpu.VMEM((8, 3, 16, 128), bf16), pltpu.VMEM((8, 3, 16, 128), bf16), pltpu.VMEM((CH, 16, 128), f32),
            D((3,)), D((3,)), D((16,)), D((16,)), D((16,)), D((16,)), D((8,)), D((8,)), D((8,)), D((8,)), D((16,)), D((16,)), D((16,)), D((16,)),
        ],
        compiler_params=pltpu.CompilerParams(collective_id=1, has_side_effects=True, vmem_limit_bytes=48 << 20),
    )(g, h)


WIN, SHIFT, NORM_EPS, MASKED = 7, 3, 1e-05, -1e30
LOG2E = 1.4426950408889634
HIGH = lax.Precision.HIGHEST
V = pl.BlockSpec(memory_space=pltpu.VMEM)

def index_maps():
    pw1 = np.zeros((512, 448), np.float32)
    pw2 = np.zeros((512, 192), np.float32)
    ps = np.zeros((192, 448), np.float32)
    for s in range(2):
        for i in range(14):
            for j in range(14):
                w = (s * 2 + i // 7) * 2 + j // 7
                t = 64 * w + (i % 7) * 7 + j % 7
                flat = lambda a, b: (s * 14 + a) * 16 + b
                if i < 11 and j < 11:
                    pw1[t, flat(i + 3, j + 3)] = 1
                    continue
                if i >= 11 and j < 11:
                    slot, src = s * 33 + (i - 11) * 11 + j, flat(i - 11, j + 3)
                elif i < 11:
                    slot, src = 80 + s * 33 + i * 3 + j - 11, flat(i + 3, j - 11)
                else:
                    slot, src = 160 + s * 9 + (i - 11) * 3 + j - 11, flat(i - 11, j - 11)
                pw2[t, slot] = 1
                ps[slot, src] = 1
    ea = np.zeros((2, 128, 128), np.float32)
    eb = np.zeros((56, 96), np.float32)
    er = np.zeros((96, 56), np.float32)
    for a in range(49):
        off = (a // 7) * 13 + a % 7
        ea[0, off, a] = 1
        ea[1, off, 64 + a] = 1
        eb[a, off] = 1
        er[92 - off, a] = 1
    hm = (np.arange(256)[:, None] // 64 == np.arange(128)[None, :] // 32).astype(np.float32)
    return pw1, pw2, ps, ea, eb, er, hm

def fill_flat(flat, x, u):
    flat[...] = jnp.zeros_like(flat)
    for s in range(2):
        for i in range(14):
            k = 16 * (s * 14 + i)
            flat[k:k + 14, 0:384] = x[s, i]
            flat[k:k + 14, 384:768] = u[s, i]

def dot(a, b, ca=1, cb=0, **kw):
    return lax.dot_general(a, b, (((ca,), (cb,)), ((), ())), preferred_element_type=f32, **kw)

def halo_kernel(x, u, ps, out, flat, box, ss, rs):
    row, z, scene = lax.axis_index("row"), lax.axis_index("col"), lax.axis_index("scene")
    rm, zm = lax.rem(row + 7, 8), lax.rem(z + 7, 8)
    rp, zp = lax.rem(row + 1, 8), lax.rem(z + 1, 8)
    bar = pltpu.get_barrier_semaphore()
    for d in ((rp, z, scene), (row, zp, scene), (rp, zp, scene)):
        pl.semaphore_signal(bar, inc=1, device_id=d, device_id_type=MESH)
    fill_flat(flat, x, u)
    box[...] = dot(ps[...], flat[...]).astype(bf16)
    pl.semaphore_wait(bar, 3)
    copies = []
    for i, (d, lo, n) in enumerate((((rm, z, scene), 0, 80), ((row, zm, scene), 80, 80), ((rm, zm, scene), 160, 32))):
        c = pltpu.make_async_remote_copy(src_ref=box.at[pl.ds(lo, n)], dst_ref=out.at[pl.ds(lo, n)], send_sem=ss.at[i],
                                         recv_sem=rs.at[i], device_id=d, device_id_type=MESH)
        c.start()
        copies.append(c)
    for c in copies:
        c.wait()

def halo(x, u, ps):
    return pl.pallas_call(
        halo_kernel, out_shape=jax.ShapeDtypeStruct((192, 768), bf16), in_specs=[V] * 3, out_specs=V,
        scratch_shapes=[pltpu.VMEM((448, 768), bf16), pltpu.VMEM((192, 768), bf16), pltpu.SemaphoreType.DMA((3,)), pltpu.SemaphoreType.DMA((3,))],
        compiler_params=pltpu.CompilerParams(collective_id=0, has_side_effects=True, vmem_limit_bytes=48 << 20),
    )(x, u, ps)

def bias_tables(table, ea, eb, tbl, wide):
    tt = tbl[...]
    tt[...] if False else None

def local_kernel(where, x, u, rx, gain, shift, wqkv, bqkv, wproj, table, pw1, pw2, q1, q2, ea, eb, er, hm,
                 g_out, gl_out, hs_out,
                 flat, xhat, norm, up, qkv, gat, attn, gq, tvar, gtab, tab, small, gsh):
    row, col = where()
    tab[...] = jnp.zeros_like(tab)
    tab[4:173, 0:12] = table[...] * LOG2E
    heads = tab[...].T
    for pair in range(6):
        acc = None
        for half in range(2):
            h = 2 * pair + half
            wide = jnp.broadcast_to(heads[h:h + 1], (96, 256))
            wide = pltpu.roll(wide, 168, 1, stride=1, stride_axis=0)[:, :128]
            rows = dot(eb[...], wide, precision=HIGH)
            part = dot(rows, ea[half], precision=HIGH)
            acc = part if acc is None else acc + part
        tvar[0, pair // 2, :, (pair % 2) * 128:(pair % 2) * 128 + 128] = acc
    key = lax.broadcasted_iota(jnp.int32, (56, 256), 0)
    query = lax.broadcasted_iota(jnp.int32, (56, 256), 1) & 63
    def low(t):
        return ((t >= 28).astype(jnp.int32), ((t - 7 * ((t * 37) >> 8)) >= 4).astype(jnp.int32))
    (ky, kx), (qy, qx) = low(key), low(query)
    pad = key >= 49
    bad_row = ((ky != qy) & (query < 49)) & (row == 7)
    bad_col = ((kx != qx) & (query < 49)) & (col == 7)
    for grp in range(3):
        t = jnp.where(pad, MASKED, tvar[0, grp])
        tvar[0, grp] = t
        tr = jnp.where(bad_row, MASKED, t)
        tvar[1, grp] = jnp.where(bad_col, MASKED, t)
        tvar[2, grp] = tr
        tvar[3, grp] = jnp.where(bad_col, MASKED, tr)

    fill_flat(flat, x, u)
    for half in range(2):
        lanes = slice(384 * half, 384 * half + 384)
        v = dot(pw1[...], flat[:, lanes]) + dot(pw2[...], rx[:, lanes])
        if half:
            up[...] = v.astype(bf16)
        else:
            mean = jnp.sum(v, axis=1, keepdims=True) * (1.0 / 384)
            c = v - mean
            var = jnp.sum(c * c, axis=1, keepdims=True) * (1.0 / 384)
            rstd = lax.rsqrt(var + NORM_EPS)
            xh = c * rstd
            xhat[...] = xh
            norm[...] = (xh * gain[...] + shift[...]).astype(bf16)
    for n in range(3):
        lanes = slice(384 * n, 384 * n + 384)
        qkv[:, lanes] = (dot(norm[...], wqkv[:, lanes]) + bqkv[:, lanes]).astype(bf16)
    gat[...] = dot(up[...], wproj[...], 1, 1).astype(bf16)
    gtab[...] = jnp.zeros_like(gtab)
    gq[...] = jnp.zeros_like(gq)
    scale = 32 ** -0.5
    lane = lax.broadcasted_iota(jnp.int32, (64, 128), 1)
    def merge(r):
        return jnp.where(lane < 32, r[0:64], jnp.where(lane < 64, r[64:128], jnp.where(lane < 96, r[128:192], r[192:256])))
    def window(w, carry):
        base = pl.multiple_of(w * 64, 64)
        var = lax.rem(w, 4)
        for grp in range(3):
            at_ = lambda n: slice(384 * n + 128 * grp, 384 * n + 128 * grp + 128)
            q = qkv[pl.ds(base, 64), at_(0)]
            k = qkv[pl.ds(base, 56), at_(1)]
            vv = qkv[pl.ds(base, 56), at_(2)]
            ga = gat[pl.ds(base, 64), at_(0)]
            qx = jnp.concatenate([q, q, q, q], axis=0) * hm[...]
            gx = jnp.concatenate([ga, ga, ga, ga], axis=0) * hm[...]
            s = dot(k, qx, 1, 1) * (scale * LOG2E) + tvar[var, grp]
            e = jnp.exp2(s - jnp.max(s, axis=0, keepdims=True))
            p = e * (1.0 / jnp.sum(e, axis=0, keepdims=True))
            pb = p.astype(bf16)
            attn[pl.ds(base, 64), at_(0)] = merge(dot(pb, vv, 0, 0)).astype(bf16)
            dp = dot(vv, gx, 1, 1)
            ds = p * (dp - jnp.sum(dp * p, axis=0, keepdims=True))
            gtab[grp] += ds
            db = ds.astype(bf16)
            gq[pl.ds(base, 64), at_(0)] = (merge(dot(db, k, 0, 0)) * scale).astype(bf16)
            gq[pl.ds(base, 56), at_(1)] = (dot(db, qx) * scale).astype(bf16)
            gq[pl.ds(base, 56), at_(2)] = dot(pb, gx).astype(bf16)
        return carry
    lax.fori_loop(0, 8, window, 0)

    def put(lb, m):
        for i in range(24):
            t = lb * 24 + i
            g_out[t // 9, t % 9] = m[16 * i:16 * i + 16].astype(bf16)
    for n in range(3):
        m = dot(attn[...], up[:, 128 * n:128 * n + 128], 0, 0)
        put(9 + n, m)
    for n in range(9):
        put(n, dot(norm[...], gq[:, 128 * n:128 * n + 128], 0, 0))
    ones = jnp.ones((16, 512), bf16)
    sq = dot(ones, gq[...])[0:1]
    sp = dot(ones, up[...])[0:1]
    for n in range(9):
        small[6 + n:7 + n] = sq[:, 128 * n:128 * n + 128]
    for n in range(3):
        small[15 + n:16 + n] = sp[:, 128 * n:128 * n + 128]
    for pair in range(6):
        d = gtab[pair // 2, :, (pair % 2) * 128:(pair % 2) * 128 + 128]
        for half in range(2):
            h = 2 * pair + half
            wide = dot(er[...], dot(d, ea[half], 1, 1, precision=HIGH), precision=HIGH)
            wide = jnp.concatenate([wide, jnp.zeros_like(wide)], axis=1)
            wide = pltpu.roll(wide, 248, 1, stride=1, stride_axis=0)
            u_h = jnp.sum(wide, axis=0, keepdims=True)
            small[18 + 2 * h:19 + 2 * h] = u_h[:, :128]
            small[19 + 2 * h:20 + 2 * h] = u_h[:, 128:]
    gn = dot(gq[...], wqkv[...], 1, 1).astype(bf16).astype(f32)
    xh = xhat[...]
    a = jnp.sum(gn * xh, axis=0, keepdims=True)
    b = jnp.sum(gn, axis=0, keepdims=True)
    for n in range(3):
        small[n:n + 1] = a[:, 128 * n:128 * n + 128]
        small[3 + n:4 + n] = b[:, 128 * n:128 * n + 128]
    small[42:48] = jnp.zeros((6, 128), f32)
    for c in range(32):
        if c < 6:
            t = small[8 * c:8 * c + 8]
            hi = t.astype(bf16).astype(f32)
            g_out[c, 9] = jnp.concatenate([hi, t - hi], axis=0).astype(bf16)
        else:
            g_out[c, 9] = jnp.zeros((16, 128), bf16)
    gg = gn * gain[...]
    m1 = jnp.sum(gg, axis=1, keepdims=True) * (1.0 / 384)
    m2 = jnp.sum(gg * xh, axis=1, keepdims=True) * (1.0 / 384)
    v = dot(pw1[...], flat[:, 0:384]) + dot(pw2[...], rx[:, 0:384])
    c = v - jnp.sum(v, axis=1, keepdims=True) * (1.0 / 384)
    rstd = lax.rsqrt(jnp.sum(c * c, axis=1, keepdims=True) * (1.0 / 384) + NORM_EPS)
    gsh[...] = ((gg - m1 - xh * m2) * rstd).astype(bf16)
    gl_out[...] = dot(q1[...], gsh[...]).astype(bf16)
    hs_out[...] = dot(q2[...], gsh[...]).astype(bf16)

def here():
    return lax.axis_index("row"), lax.axis_index("col")

def local(x, u, rx, gain, shift, wqkv, bqkv, wproj, table, maps, where=here):
    pw1, pw2, ps, ea, eb, er, hm = maps
    c = lambda a: jnp.asarray(a, bf16)
    S = pltpu.VMEM
    return pl.pallas_call(
        functools.partial(local_kernel, where),
        out_shape=(jax.ShapeDtypeStruct((32, 10, 16, 128), bf16), jax.ShapeDtypeStruct((448, 384), bf16), jax.ShapeDtypeStruct((192, 384), bf16)),
        in_specs=[V] * 17, out_specs=(V, V, V),
        scratch_shapes=[S((448, 768), bf16), S((512, 384), f32), S((512, 384), bf16), S((512, 384), bf16), S((512, 1152), bf16),
                        S((512, 384), bf16), S((512, 384), bf16), S((512, 1152), bf16), S((4, 3, 56, 256), f32), S((3, 56, 256), f32),
                        S((256, 128), f32), S((48, 128), f32), S((512, 384), bf16)],
        compiler_params=pltpu.CompilerParams(vmem_limit_bytes=56 << 20),
    )(x, u, rx, gain.reshape(1, -1), shift.reshape(1, -1), wqkv, bqkv.reshape(1, -1), wproj, table,
      c(pw1), c(pw2), c(pw1.T), c(pw2.T), jnp.asarray(ea), jnp.asarray(eb), jnp.asarray(er), c(hm))

def final_kernel(scale, g, u, gl, hr, q3, gx_out, a_out, b_out, wq_out, bq_out, wp_out, bp_out, t_out, small, tab):
    got = gl[...].astype(f32) + dot(q3[...], hr[...])
    for s in range(2):
        for i in range(14):
            k = 16 * (s * 14 + i)
            gx_out[s, i] = (u[s, i].astype(f32) + got[k:k + 14]).astype(bf16)
    for lb in range(12):
        dst, l = (wq_out, lb) if lb < 9 else (wp_out, lb - 9)
        for i in range(24):
            t = lb * 24 + i
            dst[16 * i:16 * i + 16, 128 * l:128 * l + 128] = g[t // 9, t % 9].astype(f32) * scale
    for c in range(6):
        t = g[c, 9].astype(f32)
        small[8 * c:8 * c + 8] = (t[:8] + t[8:]) * scale
    for n in range(3):
        a_out[:, 128 * n:128 * n + 128] = small[n:n + 1]
        b_out[:, 128 * n:128 * n + 128] = small[3 + n:4 + n]
        bp_out[:, 128 * n:128 * n + 128] = small[15 + n:16 + n]
    for n in range(9):
        bq_out[:, 128 * n:128 * n + 128] = small[6 + n:7 + n]
    tab[...] = jnp.zeros_like(tab)
    for h in range(12):
        tab[h:h + 1, 0:128] = small[18 + 2 * h:19 + 2 * h]
        tab[h:h + 1, 128:256] = small[19 + 2 * h:20 + 2 * h]
    t_out[...] = tab[...].T[0:169, 0:12]

def final(scale, g, u, gl, hr, maps):
    s = jax.ShapeDtypeStruct
    o = pl.pallas_call(
        functools.partial(final_kernel, scale),
        out_shape=(s((2, 14, 14, 384), bf16), s((1, 384), f32), s((1, 384), f32), s((384, 1152), f32), s((1, 1152), f32), s((384, 384), f32), s((1, 384), f32), s((169, 12), f32)),
        in_specs=[V] * 5, out_specs=(V,) * 8,
        scratch_shapes=[pltpu.VMEM((48, 128), f32), pltpu.VMEM((128, 256), f32)],
        compiler_params=pltpu.CompilerParams(vmem_limit_bytes=48 << 20),
    )(g, u, gl, hr, jnp.asarray(maps[2].T, bf16))
    return o

def on_device(features, grad_out, norm_gain, norm_shift, qkv_weight, qkv_bias, proj_weight, bias_table):
    maps = index_maps()
    rx = halo(features, grad_out, jnp.asarray(maps[2], bf16))
    g, gl, hs = local(features, grad_out, rx, norm_gain, norm_shift, qkv_weight, qkv_bias, proj_weight, bias_table, maps)
    g, hr = reduce_all(g, hs)
    scale = 1.0 / math.sqrt(8 * 112 * 112)
    gx, a, b, wq, bq, wp, bp, t = final(scale, g, grad_out, gl, hr, maps)
    return gx, a.reshape(-1), b.reshape(-1), wq, bq.reshape(-1), wp, bp.reshape(-1), t


def solution(mesh):
    return jax.shard_map(
        on_device,
        mesh=mesh,
        in_specs=(P("scene", "row", "col", None),) * 2 + (P(),) * 6,
        out_specs=(P("scene", "row", "col", None),) + (P(),) * 7,
        check_vma=False,
    )
```

time: 466 us -> 99.5 us (0.21); the launches traced: 461 us -> 99.2 us
  waiting for transfers between devices: 252 us -> 0 us
  Pallas kernels: 0 us -> 84 us
  blocking collectives: 75.9 us -> 0 us
  local copies, waits for them, and re-layouts: 57.5 us -> 12.1 us
  matrix products: 25.9 us -> 0 us
  other arithmetic: 21 us -> 2.4 us
  between operations: 14.8 us -> 0.75 us
  starting transfers between devices: 13.4 us -> 0 us
    psum x1 -> x0, waiting for transfers between devices: 247 us -> none  [on_device(): lax.psum((grad_gain, grad_shift, grad_wqkv, grad_bqkv, grad_wproj, grad_b...]
    pallas_call x0 -> x4, Pallas kernels: none -> 84 us  [the longest x1 42.3 us: reduce_all(): pl.pallas_call(functools.partial(reduce_kernel, stop), out_shape=(jax.Sha...]
    psum x1 -> x0, blocking collectives: 75.9 us -> none  [on_device(): lax.psum((grad_gain, grad_shift, grad_wqkv, grad_bqkv, grad_wproj, grad_b...]
    dot_general x13 -> x0, matrix products: 25.9 us -> none  [the longest x3 9.43 us: window_attention(): jnp.einsum('bqhd,bkhd->bhqk', queries, keys_all, precision=lax.Precision....]
    convert_element_type x8 -> x0, local copies, waits for them, and re-layouts: 21.6 us -> none  [the longest x2 15.4 us: window_attention(): qkv_win.astype(jnp.float32)]
    ppermute x4 -> x0, starting transfers between devices: 13.3 us -> none  [from_behind(): lax.ppermute(value, axis, [(i, (i + by) % size) for i in range(size)])]
    mul x8 -> x0, other arithmetic: 6.72 us -> none  [the longest x1 2.9 us: on_device(): total_wqkv * scale]
    slice x3 -> x0, local copies, waits for them, and re-layouts: 5.85 us -> none  [the longest x1 5.76 us: window_attention(): values = split_parts[:, :, 2]]
  transfers between devices with their start and end apart: 5 -> 0, of which waited for: 3 -> 0; matrix products, arithmetic and copies ran while one was open for 3% -> 0% of each run, Pallas kernels for 0% -> 0%
where the time goes in v1:
time: 99.5 us; the launch traced here: 99.2 us
  Pallas kernels  84 us (84%)
  local copies, waits for them, and re-layouts  12.1 us (12%)
  other arithmetic  2.4 us (2%)
    pallas_call x1, Pallas kernels, reduce_all(): pl.pallas_call(functools.partial(reduce_kernel, stop), out_shape=(jax.Sha...  42.3 us
    pallas_call x1, Pallas kernels, local(): pl.pallas_call(functools.partial(local_kernel, where), out_shape=(jax.Sha...  25.3 us
    pallas_call x1, Pallas kernels, halo(): pl.pallas_call(halo_kernel, out_shape=jax.ShapeDtypeStruct((192, 768), bf...  14.6 us
    unnamed x23, local copies, waits for them, and re-layouts  8.24 us
    pallas_call x4, other arithmetic, final(): pl.pallas_call(functools.partial(final_kernel, scale), out_shape=(s((2, 1...  2.4 us

profile of v1, /device:TPU:1, one launch (start us, length us, event | category | flops | bytes accessed | tf_op | source)
XLA Modules:
  0.0 99.2 jit_solution(11997954803164545492)
XLA Ops:
  0.6 0.0 copy-start.7
  0.6 1.3 %reshape.37.gain = f32[1,384]{1,0:T(1,128)} reshape(f32[384]{0:T(512)} %param.20) | data formatting | bytes 3072 | tf_op jit(solution)/shard_map/reshape | solution.py:391
  1.9 1.2 %reshape.38.shift = f32[1,384]{1,0:T(1,128)} reshape(f32[384]{0:T(512)} %param.21) | data formatting | bytes 3072 | tf_op jit(solution)/shard_map/reshape | solution.py:391
  3.2 1.3 %reshape.39.bqkv = f32[1,1152]{1,0:T(1,128)} reshape(f32[1152]{0:T(1024)} %param.23) | data formatting | bytes 9216 | tf_op jit(solution)/shard_map/reshape | solution.py:391
  4.5 1.5 %copy.30.table = f32[169,12]{1,0:T(8,128)} copy(f32[169,12]{0,1:T(8,128)} %param.25) | data formatting | bytes 16224 | tf_op args[7]
  5.9 1.0 %copy.29.u = bf16[2,14,14,384]{3,2,1,0:T(8,128)(2,1)S(1)} copy(bf16[2,14,14,384]{3,0,2,1:T(2,128)(2,1)} %param.19) | data formatting | bytes 602112 | tf_op args[1]
  6.9 0.0 copy-start
  6.9 1.1 %copy.28.x = bf16[2,14,14,384]{3,2,1,0:T(8,128)(2,1)S(1)} copy(bf16[2,14,14,384]{3,0,2,1:T(2,128)(2,1)} %param.18) | data formatting | bytes 602112 | tf_op args[0]
  8.1 0.0 copy-done.7
  8.1 0.0 copy-start.2
  8.1 14.6 %shard_map.233.rx = bf16[192,768]{1,0:T(8,128)(2,1)S(1)} custom-call(bf16[2,14,14,384]{3,2,1,0:T(8,128)(2,1)S(1)} %copy.28.x, bf16[2,14,14,384]{3,2,1,0:T(8,128)(2,1)S(1)} %copy.29.u, bf16[192,448]{1,0:T(8,128)(2,1)S(1)} %copy-done.7), custom_call_target="tpu_custom_call" | custom-call | tf_op jit(solution)/shard_map/pallas_call | solution.py:232
  22.7 0.0 copy-done
  22.7 0.0 copy-done.2
  22.7 0.0 copy-start.4
  22.7 0.7 copy-done.4
  23.4 0.0 copy-start.6
  23.4 25.3 %shard_map.234 = (bf16[32,10,16,128]{3,2,1,0:T(8,128)(2,1)}, bf16[448,384]{1,0:T(8,128)(2,1)}, bf16[192,384]{1,0:T(8,128)(2,1)}) custom-call(bf16[2,14,14,384]{3,2,1,0:T(8,128)(2,1)} %copy-done.2, bf16[2,14,14,384]{3,2,1,0:T(8,128)(2,1)} %copy-done, bf16[192,768]{1,0:T(8,128)(2,1)} %copy-done.4, f32[1,384]{1,0:T(1,128)} %reshape.37.gain, ...), custom_call_target="tpu_custom_call" | custom-call | tf_op jit(solution)/shard_map/pallas_call | solution.py:383
  48.8 0.0 copy-start.1
  48.8 0.0 copy-start.3
  48.8 1.4 %copy-done.3 = bf16[32,10,16,128]{3,2,1,0:T(8,128)(2,1)S(1)} copy-done((bf16[32,10,16,128]{3,2,1,0:T(8,128)(2,1)S(1)}, bf16[32,10,16,128]{3,2,1,0:T(8,128)(2,1)}, u32[]{:S(2)}) %copy-start.3) | copy-done | bytes 1310744
  50.1 0.0 copy-start.8
  50.1 0.9 copy-done.8
  51.0 0.0 copy-start.5
  51.0 42.3 %shard_map.235 = (bf16[32,10,16,128]{3,2,1,0:T(8,128)(2,1)S(1)}, bf16[192,384]{1,0:T(8,128)(2,1)S(1)}) custom-call(bf16[32,10,16,128]{3,2,1,0:T(8,128)(2,1)S(1)} %copy-done.3, bf16[192,384]{1,0:T(8,128)(2,1)S(1)} %copy-done.8), custom_call_target="tpu_custom_call" | custom-call | tf_op jit(solution)/shard_map/pallas_call | solution.py:150
  93.3 0.0 copy-done.6
  93.3 0.0 copy-done.1
  93.3 0.0 copy-done.5
  93.3 1.8 %shard_map.236 = (bf16[2,14,14,384]{3,2,1,0:T(8,128)(2,1)S(1)}, f32[1,384]{1,0:T(1,128)S(1)}, f32[1,384]{1,0:T(1,128)S(1)}, f32[384,1152]{1,0:T(8,128)}, f32[1,1...) custom-call(bf16[32,10,16,128]{3,2,1,0:T(8,128)(2,1)S(1)} %get-tuple-element.23.g, ...), custom_call_target="tpu_custom_call" | custom-call | tf_op jit(solution)/shard_map/pallas_call | solution.py:422
  95.2 0.9 copy.32
  96.1 0.6 reduce
  96.7 0.6 reduce.1
  97.3 0.6 reduce.3
  97.9 0.6 reduce.2
  98.5 0.7 copy.33
Async XLA Ops:
  0.6 7.5 %copy-start.7 = (bf16[192,448]{1,0:T(8,128)(2,1)S(1)}, bf16[192,448]{1,0:T(8,128)(2,1)}, u32[]{:S(2)}) copy-start(bf16[192,448]{1,0:T(8,128)(2,1)} %constant.20.clone.ps) | copy-start | bytes 516100
  6.9 15.8 %copy-start = (bf16[2,14,14,384]{3,2,1,0:T(8,128)(2,1)}, bf16[2,14,14,384]{3,2,1,0:T(8,128)(2,1)S(1)}, u32[]{:S(2)}) copy-start(bf16[2,14,14,384]{3,2,1,0:T(8,128)(2,1)S(1)} %copy.29.u) | copy-start | bytes 903172
  8.1 14.6 %copy-start.2 = (bf16[2,14,14,384]{3,2,1,0:T(8,128)(2,1)}, bf16[2,14,14,384]{3,2,1,0:T(8,128)(2,1)S(1)}, u32[]{:S(2)}) copy-start(bf16[2,14,14,384]{3,2,1,0:T(8,128)(2,1)S(1)} %copy.28.x) | copy-start | bytes 903172
  22.7 0.7 copy-start.4
  23.4 69.9 %copy-start.6 = (bf16[448,192]{1,0:T(8,128)(2,1)S(1)}, bf16[448,192]{1,0:T(8,128)(2,1)}, u32[]{:S(2)}) copy-start(bf16[448,192]{1,0:T(8,128)(2,1)} %constant.29.clone.q3) | copy-start | bytes 516100
  48.8 44.6 %copy-start.1 = (bf16[2,14,14,384]{3,2,1,0:T(8,128)(2,1)S(1)}, bf16[2,14,14,384]{3,2,1,0:T(8,128)(2,1)}, u32[]{:S(2)}) copy-start(bf16[2,14,14,384]{3,2,1,0:T(8,128)(2,1)} %copy-done) | copy-start | bytes 903172
  48.8 1.4 %copy-start.3 = (bf16[32,10,16,128]{3,2,1,0:T(8,128)(2,1)S(1)}, bf16[32,10,16,128]{3,2,1,0:T(8,128)(2,1)}, u32[]{:S(2)}) copy-start(bf16[32,10,16,128]{3,2,1,0:T(8,128)(2,1)} %get-tuple-element.21.g) | copy-start | bytes 3932164
  50.1 0.9 copy-start.8
  51.0 42.3 %copy-start.5 = (bf16[448,384]{1,0:T(8,128)(2,1)S(1)}, bf16[448,384]{1,0:T(8,128)(2,1)}, u32[]{:S(2)}) copy-start(bf16[448,384]{1,0:T(8,128)(2,1)} %get-tuple-element.24.gl) | copy-start | bytes 1032196

commit v2 on v0

v2 whole, which is shorter than its diff:
```python
import functools
import math

import jax
import jax.numpy as jnp
import numpy as np
from jax import lax
from jax.experimental import pallas as pl
from jax.experimental.pallas import tpu as pltpu
from jax.sharding import PartitionSpec as P

WIN, SHIFT, NORM_EPS, MASKED = 7, 3, 1e-05, -1e30
LOG2E = 1.4426950408889634
HIGH = lax.Precision.HIGHEST
MESH = pl.DeviceIdType.MESH
f32, bf16 = jnp.float32, jnp.bfloat16
V = pl.BlockSpec(memory_space=pltpu.VMEM)


def index_maps():
    pw1 = np.zeros((512, 392), np.float32)
    pw2 = np.zeros((512, 192), np.float32)
    ps = np.zeros((192, 392), np.float32)
    for s in range(2):
        for i in range(14):
            for j in range(14):
                w = (s * 2 + i // 7) * 2 + j // 7
                t = 64 * w + (i % 7) * 7 + j % 7
                flat = lambda a, b: (a * 14 + b) * 2 + s
                if i < 11 and j < 11:
                    pw1[t, flat(i + 3, j + 3)] = 1
                    continue
                if i >= 11 and j < 11:
                    slot, src = s * 33 + (i - 11) * 11 + j, flat(i - 11, j + 3)
                elif i < 11:
                    slot, src = 80 + s * 33 + i * 3 + j - 11, flat(i + 3, j - 11)
                else:
                    slot, src = 160 + s * 9 + (i - 11) * 3 + j - 11, flat(i - 11, j - 11)
                pw2[t, slot] = 1
                ps[slot, src] = 1
    ea = np.zeros((2, 128, 128), np.float32)
    eb = np.zeros((56, 96), np.float32)
    er = np.zeros((96, 56), np.float32)
    for a in range(49):
        off = (a // 7) * 13 + a % 7
        ea[0, off, a] = 1
        ea[1, off, 64 + a] = 1
        eb[a, off] = 1
        er[92 - off, a] = 1
    hm = (np.arange(256)[:, None] // 64 == np.arange(128)[None, :] // 32).astype(np.float32)
    return pw1, pw2, ps, ea, eb, er, hm


def place():
    row, z, scene = lax.axis_index("row"), lax.axis_index("col"), lax.axis_index("scene")
    x = (row // 4) * 2 + scene // 2
    return x, row % 4, z, scene % 2


def at(x, y, z, core):
    return ((x // 2) * 4 + y, z, (x % 2) * 2 + core)


def dot(a, b, ca=1, cb=0, **kw):
    return lax.dot_general(a, b, (((ca,), (cb,)), ((), ())), preferred_element_type=f32, **kw)


def split(t):
    hi = t.astype(bf16).astype(f32)
    return jnp.concatenate([hi, t - hi], axis=0).astype(bf16)


def main_kernel(
    x, u, gain, shift, wqkv, bqkv, wproj, table, pw1, pw2, ps, q1, q2, ea, eb, er, hm,
    out, gl, hout,
    flat, box, rx, xhat, rstd, norm, up, qkv, gat, attn, gq, tvar, gtab, tab, small, gsh,
    g, r0, s1, r1, acc, sg, t0, ts, t1, tacc, s2, r2, hbox,
    hs, hr, bs, br, p0s, p0r, p1s, p1r, q0s, q0r, q1s, q1r, p2s, p2r, p3s, p3r, p4s, p4r, p5s, p5r,
):
    px, py, z, core = place()
    me = px * 4 + py
    row, scene = lax.axis_index("row"), lax.axis_index("scene")
    rm, zm = lax.rem(row + 7, 8), lax.rem(z + 7, 8)
    rp, zp = lax.rem(row + 1, 8), lax.rem(z + 1, 8)
    sib = at(px, py, z, 1 - core)

    def plane(k):
        return at(lax.rem(px + k // 4, 4), lax.rem(py + k % 4, 4), z, core)

    def plane_from(k):
        return lax.rem(px + 4 - k // 4, 4) * 4 + lax.rem(py + 4 - k % 4, 4)

    def depth(k):
        return at(px, py, lax.rem(z + k, 8), core)

    def send(src, dst, ss, rs, dev):
        return pltpu.make_async_remote_copy(
            src_ref=src, dst_ref=dst, send_sem=ss, recv_sem=rs, device_id=dev, device_id_type=MESH
        )

    bar = pltpu.get_barrier_semaphore()
    peers = [sib] + [plane(k) for k in range(1, 16)] + [depth(k) for k in range(1, 8)]
    peers += [(rm, zm, scene), (rp, zp, scene)]
    for d in peers:
        pl.semaphore_signal(bar, inc=1, device_id=d, device_id_type=MESH)

    for p in range(196):
        flat[2 * p : 2 * p + 2, 0:384] = x[p]
        flat[2 * p : 2 * p + 2, 384:768] = u[p]
    box[...] = dot(ps[...], flat[...]).astype(bf16)
    pl.semaphore_wait(bar, len(peers))
    pieces = ((0, 80), (80, 80), (160, 32))
    halo = []
    for i, (d, (lo, n)) in enumerate(zip(((rm, z, scene), (row, zm, scene), (rm, zm, scene)), pieces)):
        c = send(box.at[pl.ds(lo, n)], rx.at[pl.ds(lo, n)], hs.at[i], hr.at[i], d)
        c.start()
        halo.append(c)

    tab[...] = jnp.zeros_like(tab)
    tab[0:12, 0:169] = table[...] * LOG2E
    heads = pltpu.roll(tab[...], 4, 1)
    for pair in range(6):
        parts = []
        for half in range(2):
            h = 2 * pair + half
            wide = jnp.broadcast_to(heads[h : h + 1], (96, 256))
            wide = pltpu.roll(wide, 168, 1, stride=1, stride_axis=0)[:, :128]
            rows = dot(eb[...], wide, precision=HIGH)
            parts.append(dot(rows, ea[half], precision=HIGH))
        lo = (pair % 2) * 128
        tvar[0, pair // 2, :, lo : lo + 128] = parts[0] + parts[1]
    key = lax.broadcasted_iota(jnp.int32, (56, 256), 0)
    query = lax.broadcasted_iota(jnp.int32, (56, 256), 1) & 63

    def low(t):
        return (t >= 28).astype(jnp.int32), ((t - 7 * ((t * 37) >> 8)) >= 4).astype(jnp.int32)

    (ky, kx), (qy, qx_) = low(key), low(query)
    pad = key >= 49
    bad_row = ((ky != qy) & (query < 49)) & (row == 7)
    bad_col = ((kx != qx_) & (query < 49)) & (z == 7)
    for grp in range(3):
        t = jnp.where(pad, MASKED, tvar[0, grp])
        tvar[0, grp] = t
        tr = jnp.where(bad_row, MASKED, t)
        tvar[1, grp] = jnp.where(bad_col, MASKED, t)
        tvar[2, grp] = tr
        tvar[3, grp] = jnp.where(bad_col, MASKED, tr)
    gtab[...] = jnp.zeros_like(gtab)
    gq[...] = jnp.zeros_like(gq)

    for c in halo:
        c.wait_recv()
    v = dot(pw1[...], flat[:, 384:768]) + dot(pw2[...], rx[:, 384:768])
    up[...] = v.astype(bf16)
    v = dot(pw1[...], flat[:, 0:384]) + dot(pw2[...], rx[:, 0:384])
    cen = v - jnp.sum(v, axis=1, keepdims=True) * (1.0 / 384)
    inv = lax.rsqrt(jnp.sum(cen * cen, axis=1, keepdims=True) * (1.0 / 384) + NORM_EPS)
    rstd[...] = inv
    xh = cen * inv
    xhat[...] = xh
    norm[...] = (xh * gain[...].reshape(1, 384) + shift[...].reshape(1, 384)).astype(bf16)
    for n in range(3):
        lanes = slice(384 * n, 384 * n + 384)
        qkv[:, lanes] = (dot(norm[...], wqkv[:, lanes]) + bqkv[...].reshape(1, 1152)[:, lanes]).astype(bf16)
    gat[...] = dot(up[...], wproj[...], 1, 1).astype(bf16)

    scale = 32**-0.5
    lane = lax.broadcasted_iota(jnp.int32, (64, 128), 1)

    def merge(r):
        return jnp.where(
            lane < 32, r[0:64], jnp.where(lane < 64, r[64:128], jnp.where(lane < 96, r[128:192], r[192:256]))
        )

    def window(w, carry):
        base = pl.multiple_of(w * 64, 64)
        var = lax.rem(w, 4)
        for grp in range(3):
            lanes = [slice(384 * n + 128 * grp, 384 * n + 128 * grp + 128) for n in range(3)]
            q = qkv[pl.ds(base, 64), lanes[0]]
            k = qkv[pl.ds(base, 56), lanes[1]]
            vv = qkv[pl.ds(base, 56), lanes[2]]
            ga = gat[pl.ds(base, 64), lanes[0]]
            qx = jnp.concatenate([q, q, q, q], axis=0) * hm[...]
            gx = jnp.concatenate([ga, ga, ga, ga], axis=0) * hm[...]
            s = dot(k, qx, 1, 1) * (scale * LOG2E) + tvar[var, grp]
            e = jnp.exp2(s - jnp.max(s, axis=0, keepdims=True))
            p = e * (1.0 / jnp.sum(e, axis=0, keepdims=True))
            pb = p.astype(bf16)
            attn[pl.ds(base, 64), lanes[0]] = merge(dot(pb, vv, 0, 0)).astype(bf16)
            dp = dot(vv, gx, 1, 1)
            ds = p * (dp - jnp.sum(dp * p, axis=0, keepdims=True))
            gtab[grp] += ds
            db = ds.astype(bf16)
            gq[pl.ds(base, 64), lanes[0]] = (merge(dot(db, k, 0, 0)) * scale).astype(bf16)
            gq[pl.ds(base, 56), lanes[1]] = (dot(db, qx) * scale).astype(bf16)
            gq[pl.ds(base, 56), lanes[2]] = dot(pb, gx).astype(bf16)
        return carry

    lax.fori_loop(0, 8, window, 0)

    def put(lb, m):
        for i in range(24):
            t = lb * 24 + i
            g[t // 9, t % 9] = m[16 * i : 16 * i + 16].astype(bf16)

    for n in range(3):
        m = dot(attn[...], up[:, 128 * n : 128 * n + 128], 0, 0)
        put(9 + n, m)
    for n in range(9):
        put(n, dot(norm[...], gq[:, 128 * n : 128 * n + 128], 0, 0))

    def chunk(k):
        return lax.rem(px + k // 4, 4) * 4 + lax.rem(py + k % 4, 4)

    order = list(range(1, 16)) + [0]
    c0, c1 = [None] * 16, [None] * 16
    for k in order:
        c = chunk(k)
        c0[k] = send(g.at[(1 - core) * 16 + c], r0.at[c], p0s.at[k], p0r.at[k], sib)
        c0[k].start()

    gn = dot(gq[...], wqkv[...], 1, 1).astype(bf16).astype(f32)
    xh = xhat[...]
    a = jnp.sum(gn * xh, axis=0, keepdims=True)
    b = jnp.sum(gn, axis=0, keepdims=True)
    for n in range(3):
        small[n : n + 1] = a[:, 128 * n : 128 * n + 128]
        small[3 + n : 4 + n] = b[:, 128 * n : 128 * n + 128]

    for k in order:
        c = chunk(k)
        c0[k].wait_recv()
        total = g[core * 16 + c].astype(f32) + r0[c].astype(f32)
        if k:
            s1[c] = total.astype(bf16)
            c1[k] = send(s1.at[c], r1.at[k], p1s.at[k], p1r.at[k], plane(k))
            c1[k].start()
        else:
            acc[...] = total

    gg = gn * gain[...].reshape(1, 384)
    m1 = jnp.sum(gg, axis=1, keepdims=True) * (1.0 / 384)
    m2 = jnp.sum(gg * xh, axis=1, keepdims=True) * (1.0 / 384)
    gsh[...] = ((gg - m1 - xh * m2) * rstd[...]).astype(bf16)
    hbox[...] = dot(q2[...], gsh[...]).astype(bf16)
    back = []
    for i, (d, (lo, n)) in enumerate(zip(((rp, z, scene), (row, zp, scene), (rp, zp, scene)), pieces)):
        c = send(hbox.at[pl.ds(lo, n)], hout.at[pl.ds(lo, n)], bs.at[i], br.at[i], d)
        c.start()
        back.append(c)
    gl[...] = dot(q1[...], gsh[...]).astype(bf16)

    ones = jnp.ones((16, 512), bf16)
    sq = dot(ones, gq[...])[0:1]
    sp = dot(ones, up[...])[0:1]
    for n in range(9):
        small[6 + n : 7 + n] = sq[:, 128 * n : 128 * n + 128]
    for n in range(3):
        small[15 + n : 16 + n] = sp[:, 128 * n : 128 * n + 128]
    for pair in range(6):
        lo = (pair % 2) * 128
        d = gtab[pair // 2, :, lo : lo + 128]
        for half in range(2):
            h = 2 * pair + half
            wide = dot(er[...], dot(d, ea[half], 1, 1, precision=HIGH), precision=HIGH)
            wide = jnp.concatenate([wide, jnp.zeros_like(wide)], axis=1)
            wide = pltpu.roll(wide, 248, 1, stride=1, stride_axis=0)
            u_h = jnp.sum(wide, axis=0, keepdims=True)
            small[18 + 2 * h : 19 + 2 * h] = u_h[:, :128]
            small[19 + 2 * h : 20 + 2 * h] = u_h[:, 128:]
    small[42:48] = jnp.zeros((6, 128), f32)
    for c in range(32):
        sg[c] = split(small[8 * c : 8 * c + 8]) if c < 6 else jnp.zeros((16, 128), bf16)
    d0 = send(sg.at[pl.ds((1 - core) * 16, 16)], t0, q0s, q0r, sib)
    d0.start()
    d0.wait_recv()
    d1 = [None] * 16
    for k in order:
        c = chunk(k)
        total = sg[core * 16 + c].astype(f32) + t0[c].astype(f32)
        total = total[:8] + total[8:]
        if k:
            ts[c] = split(total)
            d1[k] = send(ts.at[c], t1.at[k], q1s.at[k], q1r.at[k], plane(k))
            d1[k].start()
        else:
            tacc[...] = total

    for k in range(1, 16):
        c1[k].wait_recv()
        acc[...] += r1[k].astype(f32)
    for k in range(1, 16):
        d1[k].wait_recv()
        t = t1[k].astype(f32)
        tacc[...] += t[:8] + t[8:]

    big, little = acc[...].astype(bf16), split(tacc[...])
    for t in range(8):
        s2[t, 0] = big[t]
        s2[t, 1] = big[8]
        s2[t, 2] = little
    c2, c3, c4, c5 = [None] * 8, [None] * 8, [None] * 16, [None] * 16
    for k in range(1, 8):
        d = lax.rem(z + k, 8)
        c2[k] = send(s2.at[d], r2.at[z], p2s.at[k], p2r.at[k], depth(k))
        c2[k].start()
    r2[z] = s2[z]
    for k in range(1, 8):
        fr = lax.rem(z + 8 - k, 8)
        send(s2.at[fr], r2.at[fr], p2s.at[k], p2r.at[k], depth(k)).wait_recv()
    t3 = r2[0].astype(f32)
    for t in range(1, 8):
        t3 += r2[t].astype(f32)
    mine = core * 16 + me
    out[mine, z] = t3[0].astype(bf16)
    for k in range(1, 8):
        c3[k] = send(out.at[mine, z], out.at[mine, z], p3s.at[k], p3r.at[k], depth(k))
        c3[k].start()
    out[mine, 8] = t3[1].astype(bf16)
    out[mine, 9] = split(t3[2, :8] + t3[2, 8:])
    for k in range(1, 8):
        fr = lax.rem(z + 8 - k, 8)
        send(out.at[mine, fr], out.at[mine, fr], p3s.at[k], p3r.at[k], depth(k)).wait_recv()
    for k in range(1, 16):
        c4[k] = send(out.at[mine], out.at[mine], p4s.at[k], p4r.at[k], plane(k))
        c4[k].start()
    c5[0] = send(out.at[mine], out.at[mine], p5s.at[0], p5r.at[0], sib)
    c5[0].start()
    for k in range(1, 16):
        f = core * 16 + plane_from(k)
        send(out.at[f], out.at[f], p4s.at[k], p4r.at[k], plane(k)).wait_recv()
        c5[k] = send(out.at[f], out.at[f], p5s.at[k], p5r.at[k], sib)
        c5[k].start()
    for k in range(16):
        f = (1 - core) * 16 + plane_from(k)
        send(out.at[f], out.at[f], p5s.at[k], p5r.at[k], sib).wait_recv()
    for c in back:
        c.wait_recv()
    for c in halo + back + c0 + c1 + [d0] + d1 + c2 + c3 + c4 + c5:
        if c is not None:
            c.wait_send()


def run_main(x, u, gain, shift, wqkv, bqkv, wproj, table, maps):
    pw1, pw2, ps, ea, eb, er, hm = maps
    c = lambda a: jnp.asarray(a, bf16)
    S, s, D = pltpu.VMEM, jax.ShapeDtypeStruct, pltpu.SemaphoreType.DMA
    sems = [D((n,)) for n in (3, 3, 3, 3, 16, 16, 16, 16)] + [D(()), D(())]
    sems += [D((n,)) for n in (16, 16, 8, 8, 8, 8, 16, 16, 16, 16)]
    return pl.pallas_call(
        main_kernel,
        out_shape=(s((32, 10, 16, 128), bf16), s((392, 384), bf16), s((192, 384), bf16)),
        in_specs=[V] * 17,
        out_specs=(V, V, V),
        scratch_shapes=[
            S((392, 768), bf16), S((192, 768), bf16), S((192, 768), bf16),
            S((512, 384), f32), S((512, 1), f32), S((512, 384), bf16), S((512, 384), bf16),
            S((512, 1152), bf16), S((512, 384), bf16), S((512, 384), bf16), S((512, 1152), bf16),
            S((4, 3, 56, 256), f32), S((3, 56, 256), f32), S((16, 256), f32), S((48, 128), f32), S((512, 384), bf16),
            S((32, 9, 16, 128), bf16), S((16, 9, 16, 128), bf16), S((16, 9, 16, 128), bf16), S((16, 9, 16, 128), bf16),
            S((9, 16, 128), f32), S((32, 16, 128), bf16), S((16, 16, 128), bf16), S((16, 16, 128), bf16),
            S((16, 16, 128), bf16), S((8, 128), f32), S((8, 3, 16, 128), bf16), S((8, 3, 16, 128), bf16),
            S((192, 384), bf16),
        ] + sems,
        compiler_params=pltpu.CompilerParams(collective_id=0, has_side_effects=True, vmem_limit_bytes=50 << 20),
    )(x, u, gain, shift, wqkv, bqkv, wproj, table, c(pw1), c(pw2), c(ps), c(pw1.T), c(pw2.T),
      jnp.asarray(ea), jnp.asarray(eb), jnp.asarray(er), c(hm))


def final_kernel(scale, g, u, gl, hr, q3, gx_out, a_out, b_out, wq_out, bq_out, wp_out, bp_out, t_out, small, tab):
    got = gl[...].astype(f32) + dot(q3[...], hr[...])
    for p in range(196):
        gx_out[p] = (u[p].astype(f32) + got[2 * p : 2 * p + 2]).astype(bf16)
    for lb in range(12):
        dst, l = (wq_out, lb) if lb < 9 else (wp_out, lb - 9)
        for i in range(24):
            t = lb * 24 + i
            dst[16 * i : 16 * i + 16, 128 * l : 128 * l + 128] = g[t // 9, t % 9].astype(f32) * scale
    for c in range(6):
        t = g[c, 9].astype(f32)
        small[8 * c : 8 * c + 8] = (t[:8] + t[8:]) * scale
    for n in range(3):
        d = pl.ds(128 * n, 128)
        a_out[d] = small[n]
        b_out[d] = small[3 + n]
        bp_out[d] = small[15 + n]
    for n in range(9):
        bq_out[pl.ds(128 * n, 128)] = small[6 + n]
    tab[...] = jnp.zeros_like(tab)
    for h in range(12):
        tab[h : h + 1, 0:128] = small[18 + 2 * h : 19 + 2 * h]
        tab[h : h + 1, 128:256] = small[19 + 2 * h : 20 + 2 * h]
    t_out[...] = tab[0:12, 0:169]


def run_final(scale, g, u, gl, hr, maps):
    s = jax.ShapeDtypeStruct
    return pl.pallas_call(
        functools.partial(final_kernel, scale),
        out_shape=(
            s((196, 2, 384), bf16), s((384,), f32), s((384,), f32), s((384, 1152), f32),
            s((1152,), f32), s((384, 384), f32), s((384,), f32), s((12, 169), f32),
        ),
        in_specs=[V] * 5,
        out_specs=(V,) * 8,
        scratch_shapes=[pltpu.VMEM((48, 128), f32), pltpu.VMEM((16, 256), f32)],
        compiler_params=pltpu.CompilerParams(vmem_limit_bytes=40 << 20),
    )(g, u, gl, hr, jnp.asarray(maps[2].T, bf16))


def on_device(features, grad_out, norm_gain, norm_shift, qkv_weight, qkv_bias, proj_weight, bias_table):
    maps = index_maps()
    x = features.transpose(1, 2, 0, 3).reshape(196, 2, 384)
    u = grad_out.transpose(1, 2, 0, 3).reshape(196, 2, 384)
    g, gl, hr = run_main(x, u, norm_gain, norm_shift, qkv_weight, qkv_bias, proj_weight, bias_table.T, maps)
    scale = 1.0 / math.sqrt(8 * 112 * 112)
    gx, a, b, wq, bq, wp, bp, t = run_final(scale, g, u, gl, hr, maps)
    return gx.reshape(14, 14, 2, 384).transpose(2, 0, 1, 3), a, b, wq, bq, wp, bp, t.T


def solution(mesh):
    return jax.shard_map(
        on_device,
        mesh=mesh,
        in_specs=(P("scene", "row", "col", None),) * 2 + (P(),) * 6,
        out_specs=(P("scene", "row", "col", None),) + (P(),) * 7,
        check_vma=False,
    )
```

time: 466 us -> 89 us (0.19)
  waiting for transfers between devices: 252 us -> 0 us
  blocking collectives: 75.9 us -> 0 us
  Pallas kernels: 0 us -> 71.3 us
  local copies, waits for them, and re-layouts: 57.5 us -> 16.3 us
  matrix products: 25.9 us -> 0 us
  other arithmetic: 21 us -> 0 us
  between operations: 14.8 us -> 0.69 us
  starting transfers between devices: 13.4 us -> 0 us
    psum x1 -> x0, waiting for transfers between devices: 247 us -> none  [on_device(): lax.psum((grad_gain, grad_shift, grad_wqkv, grad_bqkv, grad_wproj, grad_b...]
    psum x1 -> x0, blocking collectives: 75.9 us -> none  [on_device(): lax.psum((grad_gain, grad_shift, grad_wqkv, grad_bqkv, grad_wproj, grad_b...]
    pallas_call x0 -> x2, Pallas kernels: none -> 71.3 us  [the longest x1 69.1 us: run_main(): pl.pallas_call(main_kernel, out_shape=(s((32, 10, 16, 128), bf16), s((392...]
    dot_general x13 -> x0, matrix products: 25.9 us -> none  [the longest x3 9.43 us: window_attention(): jnp.einsum('bqhd,bkhd->bhqk', queries, keys_all, precision=lax.Precision....]
    convert_element_type x8 -> x0, local copies, waits for them, and re-layouts: 21.6 us -> none  [the longest x2 15.4 us: window_attention(): qkv_win.astype(jnp.float32)]
    ppermute x4 -> x0, starting transfers between devices: 13.3 us -> none  [from_behind(): lax.ppermute(value, axis, [(i, (i + by) % size) for i in range(size)])]
    reshape x3 -> x0, local copies, waits for them, and re-layouts: 9.49 us -> none  [the longest x1 6.89 us: window_attention(): qkv_win.astype(jnp.float32)]
    mul x8 -> x0, other arithmetic: 6.72 us -> none  [the longest x1 2.9 us: on_device(): total_wqkv * scale]
  transfers between devices with their start and end apart: 5 -> 0, of which waited for: 3 -> 0; matrix products, arithmetic and copies ran while one was open for 3% -> 0% of each run, Pallas kernels for 0% -> 0%
where the time goes in v2:
time: 89 us; the launch traced here: 88.3 us
  Pallas kernels  71.3 us (80%)
  local copies, waits for them, and re-layouts  16.3 us (18%)
    pallas_call x1, Pallas kernels, run_main(): pl.pallas_call(main_kernel, out_shape=(s((32, 10, 16, 128), bf16), s((392...  69.1 us
    unnamed x38, local copies, waits for them, and re-layouts  16.3 us
    pallas_call x1, Pallas kernels, run_final(): pl.pallas_call(functools.partial(final_kernel, scale), out_shape=(s((196,...  2.17 us

profile of v2, /device:TPU:1, one launch (start us, length us, event | category | flops | bytes accessed | tf_op | source)
XLA Modules:
  0.0 88.3 jit_solution(6834702483094226915)
XLA Ops:
  0.6 0.0 copy-start.1
  0.6 1.0 %copy-done.1 = bf16[2,14,14,384]{3,0,2,1:T(2,128)(2,1)S(1)} copy-done((bf16[2,14,14,384]{3,0,2,1:T(2,128)(2,1)S(1)}, bf16[2,14,14,384]{3,0,2,1:T(2,128)(2,1)}, u32[]{:S(2)}) %copy-start.1) | copy-done | bytes 301080
  1.6 0.0 copy-start.2
  1.6 1.2 %copy-done.2 = bf16[384,1152]{1,0:T(8,128)(2,1)S(1)} copy-done((bf16[384,1152]{1,0:T(8,128)(2,1)S(1)}, bf16[384,1152]{1,0:T(8,128)(2,1)}, u32[]{:S(2)}) %copy-start.2) | copy-done | bytes 884760
  2.8 0.0 copy-start.3
  2.8 1.0 %copy-done.3 = bf16[512,392]{1,0:T(8,128)(2,1)S(1)} copy-done((bf16[512,392]{1,0:T(8,128)(2,1)S(1)}, bf16[512,392]{1,0:T(8,128)(2,1)}, u32[]{:S(2)}) %copy-start.3) | copy-done | bytes 401432
  3.8 0.0 copy-start.4
  3.8 1.0 %copy-done.4 = bf16[392,512]{1,0:T(8,128)(2,1)S(1)} copy-done((bf16[392,512]{1,0:T(8,128)(2,1)S(1)}, bf16[392,512]{1,0:T(8,128)(2,1)}, u32[]{:S(2)}) %copy-start.4) | copy-done | bytes 401432
  4.8 0.0 copy-start.5
  4.8 1.0 %copy-done.5 = bf16[2,14,14,384]{3,0,2,1:T(2,128)(2,1)S(1)} copy-done((bf16[2,14,14,384]{3,0,2,1:T(2,128)(2,1)S(1)}, bf16[2,14,14,384]{3,0,2,1:T(2,128)(2,1)}, u32[]{:S(2)}) %copy-start.5) | copy-done | bytes 301080
  5.8 0.0 copy-start.6
  5.8 1.0 %copy-done.6 = bf16[384,384]{1,0:T(8,128)(2,1)S(1)} copy-done((bf16[384,384]{1,0:T(8,128)(2,1)S(1)}, bf16[384,384]{1,0:T(8,128)(2,1)}, u32[]{:S(2)}) %copy-start.6) | copy-done | bytes 294936
  6.7 0.0 copy-start.7
  6.7 0.9 %copy-done.7 = bf16[512,192]{1,0:T(8,128)(2,1)S(1)} copy-done((bf16[512,192]{1,0:T(8,128)(2,1)S(1)}, bf16[512,192]{1,0:T(8,128)(2,1)}, u32[]{:S(2)}) %copy-start.7) | copy-done | bytes 196632
  7.7 0.0 copy-start.9
  7.7 0.9 %copy-done.9 = bf16[192,512]{1,0:T(8,128)(2,1)S(1)} copy-done((bf16[192,512]{1,0:T(8,128)(2,1)S(1)}, bf16[192,512]{1,0:T(8,128)(2,1)}, u32[]{:S(2)}) %copy-start.9) | copy-done | bytes 196632
  8.6 0.0 copy-start.10
  8.6 0.9 %copy-done.10 = bf16[192,392]{1,0:T(8,128)(2,1)S(1)} copy-done((bf16[192,392]{1,0:T(8,128)(2,1)S(1)}, bf16[192,392]{1,0:T(8,128)(2,1)}, u32[]{:S(2)}) %copy-start.10) | copy-done | bytes 150552
  9.5 0.0 copy-start.11
  9.5 0.9 %copy-done.11 = f32[2,128,128]{2,1,0:T(8,128)S(1)} copy-done((f32[2,128,128]{2,1,0:T(8,128)S(1)}, f32[2,128,128]{2,1,0:T(8,128)}, u32[]{:S(2)}) %copy-start.11) | copy-done | bytes 131096
  10.4 0.0 copy-start.12
  10.4 0.8 copy-done.12
  11.3 0.0 copy-start.13
  11.3 0.8 copy-done.13
  12.1 0.0 copy-start.14
  12.1 0.7 copy-done.14
  12.8 0.0 copy-start.15
  12.8 0.7 copy-done.15
  13.6 0.0 copy-start.16
  13.6 0.7 copy-done.16
  14.2 0.0 copy-start.17
  14.3 0.7 copy-done.17
  14.9 0.0 copy-start.18
  14.9 0.7 copy-done.18
  15.6 0.0 copy-start.8
  15.6 69.1 %shard_map.233 = (bf16[32,10,16,128]{3,2,1,0:T(8,128)(2,1)}, bf16[392,384]{1,0:T(8,128)(2,1)S(1)}, bf16[192,384]{1,0:T(8,128)(2,1)S(1)}) custom-call(bf16[196,2,384]{2,1,0:T(2,128)(2,1)S(1)} %bitcast.13, bf16[196,2,384]{2,1,0:T(2,128)(2,1)S(1)} %bitcast.11, f32[384]{0:T(512)S(1)} %copy-done.17, f32[384]{0:T(512)S(1)} %copy-done.18, ...), custom_call_target="tpu_custom_call" | custom-call | tf_op jit(solution)/shard_map/pallas_call | solution.py:352
  84.8 0.0 copy-done.8
  84.8 0.0 copy-start
  84.8 1.3 %copy-done = bf16[32,10,16,128]{3,2,1,0:T(8,128)(2,1)S(1)} copy-done((bf16[32,10,16,128]{3,2,1,0:T(8,128)(2,1)S(1)}, bf16[32,10,16,128]{3,2,1,0:T(8,128)(2,1)}, u32[]{:S(2)}) %copy-start) | copy-done | bytes 1310744
  86.1 2.2 %shard_map.234 = (bf16[196,2,384]{2,1,0:T(2,128)(2,1)}, f32[384]{0:T(512)}, f32[384]{0:T(512)}, f32[384,1152]{1,0:T(8,128)}, f32[1152]{0:T(1024)}, /*index=5*/f3...) custom-call(bf16[32,10,16,128]{3,2,1,0:T(8,128)(2,1)S(1)} %copy-done, bf16[196,2,384]{2,1,0:T(2,128)(2,1)S(1)} %bitcast.12, ...), custom_call_target="tpu_custom_call" | custom-call | tf_op jit(solution)/shard_map/pallas_call | solution.py:400
Async XLA Ops:
  0.6 1.0 %copy-start.1 = (bf16[2,14,14,384]{3,0,2,1:T(2,128)(2,1)S(1)}, bf16[2,14,14,384]{3,0,2,1:T(2,128)(2,1)}, u32[]{:S(2)}) copy-start(bf16[2,14,14,384]{3,0,2,1:T(2,128)(2,1)} %param.19) | copy-start | bytes 903172
  1.6 1.2 %copy-start.2 = (bf16[384,1152]{1,0:T(8,128)(2,1)S(1)}, bf16[384,1152]{1,0:T(8,128)(2,1)}, u32[]{:S(2)}) copy-start(bf16[384,1152]{1,0:T(8,128)(2,1)} %wqkv.1) | copy-start | bytes 2654212
  2.8 1.0 %copy-start.3 = (bf16[512,392]{1,0:T(8,128)(2,1)S(1)}, bf16[512,392]{1,0:T(8,128)(2,1)}, u32[]{:S(2)}) copy-start(bf16[512,392]{1,0:T(8,128)(2,1)} %constant.20.clone.pw1) | copy-start | bytes 1204228
  3.8 1.0 %copy-start.4 = (bf16[392,512]{1,0:T(8,128)(2,1)S(1)}, bf16[392,512]{1,0:T(8,128)(2,1)}, u32[]{:S(2)}) copy-start(bf16[392,512]{1,0:T(8,128)(2,1)} %constant.23.clone.q1) | copy-start | bytes 1204228
  4.8 1.0 %copy-start.5 = (bf16[2,14,14,384]{3,0,2,1:T(2,128)(2,1)S(1)}, bf16[2,14,14,384]{3,0,2,1:T(2,128)(2,1)}, u32[]{:S(2)}) copy-start(bf16[2,14,14,384]{3,0,2,1:T(2,128)(2,1)} %param.18) | copy-start | bytes 903172
  5.8 1.0 %copy-start.6 = (bf16[384,384]{1,0:T(8,128)(2,1)S(1)}, bf16[384,384]{1,0:T(8,128)(2,1)}, u32[]{:S(2)}) copy-start(bf16[384,384]{1,0:T(8,128)(2,1)} %wproj.1) | copy-start | bytes 884740
  6.7 0.9 %copy-start.7 = (bf16[512,192]{1,0:T(8,128)(2,1)S(1)}, bf16[512,192]{1,0:T(8,128)(2,1)}, u32[]{:S(2)}) copy-start(bf16[512,192]{1,0:T(8,128)(2,1)} %constant.21.clone.pw2) | copy-start | bytes 589828
  7.7 0.9 %copy-start.9 = (bf16[192,512]{1,0:T(8,128)(2,1)S(1)}, bf16[192,512]{1,0:T(8,128)(2,1)}, u32[]{:S(2)}) copy-start(bf16[192,512]{1,0:T(8,128)(2,1)} %constant.24.clone.q2) | copy-start | bytes 589828
  8.6 0.9 %copy-start.10 = (bf16[192,392]{1,0:T(8,128)(2,1)S(1)}, bf16[192,392]{1,0:T(8,128)(2,1)}, u32[]{:S(2)}) copy-start(bf16[192,392]{1,0:T(8,128)(2,1)} %constant.22.clone.ps) | copy-start | bytes 451588
  9.5 0.9 %copy-start.11 = (f32[2,128,128]{2,1,0:T(8,128)S(1)}, f32[2,128,128]{2,1,0:T(8,128)}, u32[]{:S(2)}) copy-start(f32[2,128,128]{2,1,0:T(8,128)} %constant.25.clone.ea) | copy-start | bytes 393220
  10.4 0.8 copy-start.12
  11.3 0.8 copy-start.13
  12.1 0.7 copy-start.14
  12.8 0.7 copy-start.15
  13.6 0.7 copy-start.16
  14.2 0.7 copy-start.17
  14.9 0.7 copy-start.18
  15.6 69.1 %copy-start.8 = (bf16[392,192]{1,0:T(8,128)(2,1)S(1)}, bf16[392,192]{1,0:T(8,128)(2,1)}, u32[]{:S(2)}) copy-start(bf16[392,192]{1,0:T(8,128)(2,1)} %constant.29.clone.q3) | copy-start | bytes 451588
  84.8 1.3 %copy-start = (bf16[32,10,16,128]{3,2,1,0:T(8,128)(2,1)S(1)}, bf16[32,10,16,128]{3,2,1,0:T(8,128)(2,1)}, u32[]{:S(2)}) copy-start(bf16[32,10,16,128]{3,2,1,0:T(8,128)(2,1)} %get-tuple-element.19.g) | copy-start | bytes 3932164

commit v3 on v2

--- a/solution.py
+++ b/solution.py
@@ -11,6 +11,7 @@
 
 WIN, SHIFT, NORM_EPS, MASKED = 7, 3, 1e-05, -1e30
 LOG2E = 1.4426950408889634
+UNROLL = 4
 HIGH = lax.Precision.HIGHEST
 MESH = pl.DeviceIdType.MESH
 f32, bf16 = jnp.float32, jnp.bfloat16
@@ -71,11 +72,13 @@
 
 
 def main_kernel(
-    x, u, gain, shift, wqkv, bqkv, wproj, table, pw1, pw2, ps, q1, q2, ea, eb, er, hm,
-    out, gl, hout,
+    x_in, u_in, ps_in, pw1_in, table_in, eb_in, ea_in, gain_in, shift_in, wqkv_in, bqkv_in, wproj_in, pw2_in, hm_in,
+    q2_in, q1_in, er_in,
+    out0, out1, out2, gl, hout,
+    x, u, ps, pw1, table, eb, ea, gain, shift, wqkv, bqkv, wproj, pw2, hm, q2, q1, er, load,
     flat, box, rx, xhat, rstd, norm, up, qkv, gat, attn, gq, tvar, gtab, tab, small, gsh,
-    g, r0, s1, r1, acc, sg, t0, ts, t1, tacc, s2, r2, hbox,
-    hs, hr, bs, br, p0s, p0r, p1s, p1r, q0s, q0r, q1s, q1r, p2s, p2r, p3s, p3r, p4s, p4r, p5s, p5r,
+    g, r0, s1, r1_0, r1_1, r1_2, acc, sg, t0, ts, t1, tacc, s2_0, s2_1, s2_2, hbox,
+    hs, hr, bs, br, p0s, p0r, p1s, p1r, q0s, q0r, q1s, q1r, p2s, p2r, p4s, p4r, p5s, p5r,
 ):
     px, py, z, core = place()
     me = px * 4 + py
@@ -104,17 +107,36 @@
     for d in peers:
         pl.semaphore_signal(bar, inc=1, device_id=d, device_id_type=MESH)
 
+    loads = [
+        pltpu.make_async_copy(a, b, load.at[i])
+        for i, (a, b) in enumerate(
+            (
+                (x_in, x), (u_in, u), (ps_in, ps), (pw1_in, pw1), (table_in, table), (eb_in, eb), (ea_in, ea),
+                (gain_in, gain), (shift_in, shift), (wqkv_in, wqkv), (bqkv_in, bqkv), (wproj_in, wproj),
+                (pw2_in, pw2), (hm_in, hm), (q2_in, q2), (q1_in, q1), (er_in, er),
+            )
+        )
+    ]
+    for c in loads:
+        c.start()
+    for c in loads[:3]:
+        c.wait()
     for p in range(196):
         flat[2 * p : 2 * p + 2, 0:384] = x[p]
         flat[2 * p : 2 * p + 2, 384:768] = u[p]
-    box[...] = dot(ps[...], flat[...]).astype(bf16)
+    box[0] = dot(ps[...], flat[:, 0:384]).astype(bf16)
+    box[1] = dot(ps[...], flat[:, 384:768]).astype(bf16)
     pl.semaphore_wait(bar, len(peers))
     pieces = ((0, 80), (80, 80), (160, 32))
     halo = []
-    for i, (d, (lo, n)) in enumerate(zip(((rm, z, scene), (row, zm, scene), (rm, zm, scene)), pieces)):
-        c = send(box.at[pl.ds(lo, n)], rx.at[pl.ds(lo, n)], hs.at[i], hr.at[i], d)
-        c.start()
-        halo.append(c)
+    for h in range(2):
+        for i, (d, (lo, n)) in enumerate(zip(((rm, z, scene), (row, zm, scene), (rm, zm, scene)), pieces)):
+            i = 3 * h + i
+            c = send(box.at[h, pl.ds(lo, n)], rx.at[h, pl.ds(lo, n)], hs.at[i], hr.at[i], d)
+            c.start()
+            halo.append(c)
+    for c in loads[3:]:
+        c.wait()
 
     tab[...] = jnp.zeros_like(tab)
     tab[0:12, 0:169] = table[...] * LOG2E
@@ -149,11 +171,10 @@
     gtab[...] = jnp.zeros_like(gtab)
     gq[...] = jnp.zeros_like(gq)
 
-    for c in halo:
+    v = dot(pw1[...], flat[:, 0:384])
+    for c in halo[:3]:
         c.wait_recv()
-    v = dot(pw1[...], flat[:, 384:768]) + dot(pw2[...], rx[:, 384:768])
-    up[...] = v.astype(bf16)
-    v = dot(pw1[...], flat[:, 0:384]) + dot(pw2[...], rx[:, 0:384])
+    v = v + dot(pw2[...], rx[0])
     cen = v - jnp.sum(v, axis=1, keepdims=True) * (1.0 / 384)
     inv = lax.rsqrt(jnp.sum(cen * cen, axis=1, keepdims=True) * (1.0 / 384) + NORM_EPS)
     rstd[...] = inv
@@ -163,6 +184,10 @@
     for n in range(3):
         lanes = slice(384 * n, 384 * n + 384)
         qkv[:, lanes] = (dot(norm[...], wqkv[:, lanes]) + bqkv[...].reshape(1, 1152)[:, lanes]).astype(bf16)
+    v = dot(pw1[...], flat[:, 384:768])
+    for c in halo[3:]:
+        c.wait_recv()
+    up[...] = (v + dot(pw2[...], rx[1])).astype(bf16)
     gat[...] = dot(up[...], wproj[...], 1, 1).astype(bf16)
 
     scale = 32**-0.5
@@ -198,28 +223,92 @@
             gq[pl.ds(base, 56), lanes[2]] = dot(pb, gx).astype(bf16)
         return carry
 
-    lax.fori_loop(0, 8, window, 0)
-
-    def put(lb, m):
-        for i in range(24):
-            t = lb * 24 + i
-            g[t // 9, t % 9] = m[16 * i : 16 * i + 16].astype(bf16)
-
-    for n in range(3):
-        m = dot(attn[...], up[:, 128 * n : 128 * n + 128], 0, 0)
-        put(9 + n, m)
-    for n in range(9):
-        put(n, dot(norm[...], gq[:, 128 * n : 128 * n + 128], 0, 0))
+    def windows(i, carry):
+        for j in range(UNROLL):
+            window(i * UNROLL + j, carry)
+        return carry
+
+    lax.fori_loop(0, 8 // UNROLL, windows, 0)
+
+    out, r1, s2 = (out0, out1, out2), (r1_0, r1_1, r1_2), (s2_0, s2_1, s2_2)
+    order = list(range(1, 16)) + [0]
+    c0, c1, c2, c4, c5, d1 = [], [], [], [], [], [None] * 16
 
     def chunk(k):
         return lax.rem(px + k // 4, 4) * 4 + lax.rem(py + k % 4, 4)
 
-    order = list(range(1, 16)) + [0]
-    c0, c1 = [None] * 16, [None] * 16
-    for k in order:
-        c = chunk(k)
-        c0[k] = send(g.at[(1 - core) * 16 + c], r0.at[c], p0s.at[k], p0r.at[k], sib)
-        c0[k].start()
+    for seg in range(3):
+        for n in range(4):
+            lb = 4 * seg + n
+            if lb < 3:
+                m = dot(attn[...], up[:, 128 * lb : 128 * lb + 128], 0, 0)
+            else:
+                m = dot(norm[...], gq[:, 128 * (lb - 3) : 128 * (lb - 3) + 128], 0, 0)
+            for i in range(24):
+                t = n * 24 + i
+                g[seg, t // 3, t % 3] = m[16 * i : 16 * i + 16].astype(bf16)
+        c = send(g.at[seg, pl.ds((1 - core) * 16, 16)], r0.at[seg], p0s.at[seg], p0r.at[seg], sib)
+        c.start()
+        c0.append(c)
+
+    def spread(seg):
+        c0[seg].wait_recv()
+        cs = [None] * 16
+        for k in order:
+            c = chunk(k)
+            total = g[seg, core * 16 + c].astype(f32) + r0[seg, c].astype(f32)
+            if k:
+                s1[seg, c] = total.astype(bf16)
+                cs[k] = send(s1.at[seg, c], r1[seg].at[k], p1s.at[seg, k], p1r.at[seg, k], plane(k))
+                cs[k].start()
+            else:
+                acc[seg] = total
+        c1.append(cs)
+
+    def deepen(seg):
+        a = acc[seg]
+        for k in range(1, 16):
+            c1[seg][k].wait_recv()
+            a = a + r1[seg][k].astype(f32)
+        s2[seg][z, 0:3] = a.astype(bf16)
+        if seg == 2:
+            for k in range(1, 16):
+                d1[k].wait_recv()
+                t = t1[k].astype(f32)
+                tacc[...] += t[:8] + t[8:]
+            s2[seg][z, 3] = split(tacc[...])
+        cs = []
+        for k in range(1, 8):
+            c = send(s2[seg].at[z], s2[seg].at[z], p2s.at[seg, k], p2r.at[seg, k], depth(k))
+            c.start()
+            cs.append(c)
+        c2.append(cs)
+
+    mine = core * 16 + me
+
+    def finish(seg):
+        for k in range(1, 8):
+            fr = lax.rem(z + 8 - k, 8)
+            send(s2[seg].at[fr], s2[seg].at[fr], p2s.at[seg, k], p2r.at[seg, k], depth(k)).wait_recv()
+        a = s2[seg][0].astype(f32)
+        for t in range(1, 8):
+            a = a + s2[seg][t].astype(f32)
+        out[seg][mine, 0:3] = a[0:3].astype(bf16)
+        if seg == 2:
+            out[seg][mine, 3] = split(a[3, :8] + a[3, 8:])
+        for k in range(1, 16):
+            c = send(out[seg].at[mine], out[seg].at[mine], p4s.at[seg, k], p4r.at[seg, k], plane(k))
+            c.start()
+            c4.append(c)
+
+    def hand_over(seg):
+        for k in range(1, 16):
+            f = core * 16 + plane_from(k)
+            send(out[seg].at[f], out[seg].at[f], p4s.at[seg, k], p4r.at[seg, k], plane(k)).wait_recv()
+        half = pl.ds(core * 16, 16)
+        c = send(out[seg].at[half], out[seg].at[half], p5s.at[seg], p5r.at[seg], sib)
+        c.start()
+        c5.append(c)
 
     gn = dot(gq[...], wqkv[...], 1, 1).astype(bf16).astype(f32)
     xh = xhat[...]
@@ -229,16 +318,8 @@
         small[n : n + 1] = a[:, 128 * n : 128 * n + 128]
         small[3 + n : 4 + n] = b[:, 128 * n : 128 * n + 128]
 
-    for k in order:
-        c = chunk(k)
-        c0[k].wait_recv()
-        total = g[core * 16 + c].astype(f32) + r0[c].astype(f32)
-        if k:
-            s1[c] = total.astype(bf16)
-            c1[k] = send(s1.at[c], r1.at[k], p1s.at[k], p1r.at[k], plane(k))
-            c1[k].start()
-        else:
-            acc[...] = total
+    for seg in range(3):
+        spread(seg)
 
     gg = gn * gain[...].reshape(1, 384)
     m1 = jnp.sum(gg, axis=1, keepdims=True) * (1.0 / 384)
@@ -259,13 +340,18 @@
         small[6 + n : 7 + n] = sq[:, 128 * n : 128 * n + 128]
     for n in range(3):
         small[15 + n : 16 + n] = sp[:, 128 * n : 128 * n + 128]
+    d = jnp.concatenate([gtab[p // 2, :, (p % 2) * 128 : (p % 2) * 128 + 128] for p in range(6)], axis=0)
+    hi = d.astype(bf16)
+    lo = (d - hi.astype(f32)).astype(bf16)
+    eab = jnp.concatenate([ea[0], ea[1]], axis=0).astype(bf16)
+    erb = er[...].astype(bf16)
+    hi, lo = dot(hi, eab, 1, 1).astype(bf16), dot(lo, eab, 1, 1).astype(bf16)
     for pair in range(6):
-        lo = (pair % 2) * 128
-        d = gtab[pair // 2, :, lo : lo + 128]
+        rows = slice(56 * pair, 56 * pair + 56)
+        r = dot(erb, hi[rows]) + dot(erb, lo[rows])
         for half in range(2):
             h = 2 * pair + half
-            wide = dot(er[...], dot(d, ea[half], 1, 1, precision=HIGH), precision=HIGH)
-            wide = jnp.concatenate([wide, jnp.zeros_like(wide)], axis=1)
+            wide = jnp.concatenate([r[:, 128 * half : 128 * half + 128], jnp.zeros((96, 128), f32)], axis=1)
             wide = pltpu.roll(wide, 248, 1, stride=1, stride_axis=0)
             u_h = jnp.sum(wide, axis=0, keepdims=True)
             small[18 + 2 * h : 19 + 2 * h] = u_h[:, :128]
@@ -275,8 +361,8 @@
         sg[c] = split(small[8 * c : 8 * c + 8]) if c < 6 else jnp.zeros((16, 128), bf16)
     d0 = send(sg.at[pl.ds((1 - core) * 16, 16)], t0, q0s, q0r, sib)
     d0.start()
+    deepen(0)
     d0.wait_recv()
-    d1 = [None] * 16
     for k in order:
         c = chunk(k)
         total = sg[core * 16 + c].astype(f32) + t0[c].astype(f32)
@@ -287,58 +373,20 @@
             d1[k].start()
         else:
             tacc[...] = total
-
-    for k in range(1, 16):
-        c1[k].wait_recv()
-        acc[...] += r1[k].astype(f32)
-    for k in range(1, 16):
-        d1[k].wait_recv()
-        t = t1[k].astype(f32)
-        tacc[...] += t[:8] + t[8:]
-
-    big, little = acc[...].astype(bf16), split(tacc[...])
-    for t in range(8):
-        s2[t, 0] = big[t]
-        s2[t, 1] = big[8]
-        s2[t, 2] = little
-    c2, c3, c4, c5 = [None] * 8, [None] * 8, [None] * 16, [None] * 16
-    for k in range(1, 8):
-        d = lax.rem(z + k, 8)
-        c2[k] = send(s2.at[d], r2.at[z], p2s.at[k], p2r.at[k], depth(k))
-        c2[k].start()
-    r2[z] = s2[z]
-    for k in range(1, 8):
-        fr = lax.rem(z + 8 - k, 8)
-        send(s2.at[fr], r2.at[fr], p2s.at[k], p2r.at[k], depth(k)).wait_recv()
-    t3 = r2[0].astype(f32)
-    for t in range(1, 8):
-        t3 += r2[t].astype(f32)
-    mine = core * 16 + me
-    out[mine, z] = t3[0].astype(bf16)
-    for k in range(1, 8):
-        c3[k] = send(out.at[mine, z], out.at[mine, z], p3s.at[k], p3r.at[k], depth(k))
-        c3[k].start()
-    out[mine, 8] = t3[1].astype(bf16)
-    out[mine, 9] = split(t3[2, :8] + t3[2, 8:])
-    for k in range(1, 8):
-        fr = lax.rem(z + 8 - k, 8)
-        send(out.at[mine, fr], out.at[mine, fr], p3s.at[k], p3r.at[k], depth(k)).wait_recv()
-    for k in range(1, 16):
-        c4[k] = send(out.at[mine], out.at[mine], p4s.at[k], p4r.at[k], plane(k))
-        c4[k].start()
-    c5[0] = send(out.at[mine], out.at[mine], p5s.at[0], p5r.at[0], sib)
-    c5[0].start()
-    for k in range(1, 16):
-        f = core * 16 + plane_from(k)
-        send(out.at[f], out.at[f], p4s.at[k], p4r.at[k], plane(k)).wait_recv()
-        c5[k] = send(out.at[f], out.at[f], p5s.at[k], p5r.at[k], sib)
-        c5[k].start()
-    for k in range(16):
-        f = (1 - core) * 16 + plane_from(k)
-        send(out.at[f], out.at[f], p5s.at[k], p5r.at[k], sib).wait_recv()
+    deepen(1)
+    finish(0)
+    deepen(2)
+    finish(1)
+    hand_over(0)
+    finish(2)
+    hand_over(1)
+    hand_over(2)
+    for seg in range(3):
+        other = pl.ds((1 - core) * 16, 16)
+        send(out[seg].at[other], out[seg].at[other], p5s.at[seg], p5r.at[seg], sib).wait_recv()
     for c in back:
         c.wait_recv()
-    for c in halo + back + c0 + c1 + [d0] + d1 + c2 + c3 + c4 + c5:
+    for c in halo + back + c0 + c1[0] + c1[1] + c1[2] + [d0] + d1 + c2[0] + c2[1] + c2[2] + c4 + c5:
         if c is not None:
             c.wait_send()
 
@@ -347,39 +395,51 @@
     pw1, pw2, ps, ea, eb, er, hm = maps
     c = lambda a: jnp.asarray(a, bf16)
     S, s, D = pltpu.VMEM, jax.ShapeDtypeStruct, pltpu.SemaphoreType.DMA
-    sems = [D((n,)) for n in (3, 3, 3, 3, 16, 16, 16, 16)] + [D(()), D(())]
-    sems += [D((n,)) for n in (16, 16, 8, 8, 8, 8, 16, 16, 16, 16)]
+    sems = [D((n,)) for n in (6, 6, 3, 3, 3, 3)] + [D((3, 16)), D((3, 16)), D(()), D(()), D((16,)), D((16,))]
+    sems += [D((3, 8)), D((3, 8)), D((3, 16)), D((3, 16)), D((3,)), D((3,))]
+    j = jnp.asarray
+    args = (x, u, c(ps), c(pw1), table, j(eb), j(ea), gain, shift, wqkv, bqkv, wproj, c(pw2), c(hm), c(pw2.T), c(pw1.T), j(er))
     return pl.pallas_call(
         main_kernel,
-        out_shape=(s((32, 10, 16, 128), bf16), s((392, 384), bf16), s((192, 384), bf16)),
-        in_specs=[V] * 17,
-        out_specs=(V, V, V),
-        scratch_shapes=[
-            S((392, 768), bf16), S((192, 768), bf16), S((192, 768), bf16),
+        out_shape=tuple(s((32, n, 16, 128), bf16) for n in (3, 3, 4)) + (s((392, 384), bf16), s((192, 384), bf16)),
+        in_specs=[pl.BlockSpec(memory_space=pltpu.HBM)] * 17,
+        out_specs=(V,) * 5,
+        scratch_shapes=[S(a.shape, a.dtype) for a in args] + [D((17,))] + [
+            S((392, 768), bf16), S((2, 192, 384), bf16), S((2, 192, 384), bf16),
             S((512, 384), f32), S((512, 1), f32), S((512, 384), bf16), S((512, 384), bf16),
             S((512, 1152), bf16), S((512, 384), bf16), S((512, 384), bf16), S((512, 1152), bf16),
             S((4, 3, 56, 256), f32), S((3, 56, 256), f32), S((16, 256), f32), S((48, 128), f32), S((512, 384), bf16),
-            S((32, 9, 16, 128), bf16), S((16, 9, 16, 128), bf16), S((16, 9, 16, 128), bf16), S((16, 9, 16, 128), bf16),
-            S((9, 16, 128), f32), S((32, 16, 128), bf16), S((16, 16, 128), bf16), S((16, 16, 128), bf16),
-            S((16, 16, 128), bf16), S((8, 128), f32), S((8, 3, 16, 128), bf16), S((8, 3, 16, 128), bf16),
-            S((192, 384), bf16),
-        ] + sems,
-        compiler_params=pltpu.CompilerParams(collective_id=0, has_side_effects=True, vmem_limit_bytes=50 << 20),
-    )(x, u, gain, shift, wqkv, bqkv, wproj, table, c(pw1), c(pw2), c(ps), c(pw1.T), c(pw2.T),
-      jnp.asarray(ea), jnp.asarray(eb), jnp.asarray(er), c(hm))
-
-
-def final_kernel(scale, g, u, gl, hr, q3, gx_out, a_out, b_out, wq_out, bq_out, wp_out, bp_out, t_out, small, tab):
+            S((3, 32, 3, 16, 128), bf16), S((3, 16, 3, 16, 128), bf16), S((3, 16, 3, 16, 128), bf16),
+        ] + [S((16, 3, 16, 128), bf16)] * 3 + [
+            S((3, 3, 16, 128), f32), S((32, 16, 128), bf16), S((16, 16, 128), bf16), S((16, 16, 128), bf16),
+            S((16, 16, 128), bf16), S((8, 128), f32),
+        ] + [S((8, n, 16, 128), bf16) for n in (3, 3, 4)] + [S((192, 384), bf16)] + sems,
+        compiler_params=pltpu.CompilerParams(collective_id=0, has_side_effects=True, vmem_limit_bytes=62 << 20),
+    )(*args)
+
+
+def final_kernel(
+    scale, g0_in, g1_in, g2_in, u_in, gl_in, hr_in, q3_in,
+    gx_out, a_out, b_out, wq_out, bq_out, wp_out, bp_out, t_out,
+    g0, g1, g2, u, gl, hr, q3, load, small, tab,
+):
+    pairs = ((g0_in, g0), (g1_in, g1), (g2_in, g2), (u_in, u), (gl_in, gl), (hr_in, hr), (q3_in, q3))
+    loads = [pltpu.make_async_copy(a, b, load.at[i]) for i, (a, b) in enumerate(pairs)]
+    for c in loads:
+        c.start()
+    for c in loads:
+        c.wait()
     got = gl[...].astype(f32) + dot(q3[...], hr[...])
     for p in range(196):
         gx_out[p] = (u[p].astype(f32) + got[2 * p : 2 * p + 2]).astype(bf16)
     for lb in range(12):
-        dst, l = (wq_out, lb) if lb < 9 else (wp_out, lb - 9)
+        dst, l = (wp_out, lb) if lb < 3 else (wq_out, lb - 3)
+        g = (g0, g1, g2)[lb // 4]
         for i in range(24):
-            t = lb * 24 + i
-            dst[16 * i : 16 * i + 16, 128 * l : 128 * l + 128] = g[t // 9, t % 9].astype(f32) * scale
+            t = (lb % 4) * 24 + i
+            dst[16 * i : 16 * i + 16, 128 * l : 128 * l + 128] = g[t // 3, t % 3].astype(f32) * scale
     for c in range(6):
-        t = g[c, 9].astype(f32)
+        t = g2[c, 3].astype(f32)
         small[8 * c : 8 * c + 8] = (t[:8] + t[8:]) * scale
     for n in range(3):
         d = pl.ds(128 * n, 128)
@@ -395,28 +455,30 @@
     t_out[...] = tab[0:12, 0:169]
 
 
-def run_final(scale, g, u, gl, hr, maps):
+def run_final(scale, g0, g1, g2, u, gl, hr, maps):
     s = jax.ShapeDtypeStruct
+    args = (g0, g1, g2, u, gl, hr, jnp.asarray(maps[2].T, bf16))
     return pl.pallas_call(
         functools.partial(final_kernel, scale),
         out_shape=(
             s((196, 2, 384), bf16), s((384,), f32), s((384,), f32), s((384, 1152), f32),
             s((1152,), f32), s((384, 384), f32), s((384,), f32), s((12, 169), f32),
         ),
-        in_specs=[V] * 5,
+        in_specs=[pl.BlockSpec(memory_space=pltpu.HBM)] * 7,
         out_specs=(V,) * 8,
-        scratch_shapes=[pltpu.VMEM((48, 128), f32), pltpu.VMEM((16, 256), f32)],
-        compiler_params=pltpu.CompilerParams(vmem_limit_bytes=40 << 20),
-    )(g, u, gl, hr, jnp.asarray(maps[2].T, bf16))
+        scratch_shapes=[pltpu.VMEM(a.shape, a.dtype) for a in args]
+        + [pltpu.SemaphoreType.DMA((7,)), pltpu.VMEM((48, 128), f32), pltpu.VMEM((16, 256), f32)],
+        compiler_params=pltpu.CompilerParams(vmem_limit_bytes=62 << 20),
+    )(*args)
 
 
 def on_device(features, grad_out, norm_gain, norm_shift, qkv_weight, qkv_bias, proj_weight, bias_table):
     maps = index_maps()
     x = features.transpose(1, 2, 0, 3).reshape(196, 2, 384)
     u = grad_out.transpose(1, 2, 0, 3).reshape(196, 2, 384)
-    g, gl, hr = run_main(x, u, norm_gain, norm_shift, qkv_weight, qkv_bias, proj_weight, bias_table.T, maps)
+    g0, g1, g2, gl, hr = run_main(x, u, norm_gain, norm_shift, qkv_weight, qkv_bias, proj_weight, bias_table.T, maps)
     scale = 1.0 / math.sqrt(8 * 112 * 112)
-    gx, a, b, wq, bq, wp, bp, t = run_final(scale, g, u, gl, hr, maps)
+    gx, a, b, wq, bq, wp, bp, t = run_final(scale, g0, g1, g2, u, gl, hr, maps)
     return gx.reshape(14, 14, 2, 384).transpose(2, 0, 1, 3), a, b, wq, bq, wp, bp, t.T
 
 

time: 89 us -> 65.8 us (0.74)
  local copies, waits for them, and re-layouts: 16.3 us -> 0 us
  Pallas kernels: 71.3 us -> 64.9 us
    unnamed x38 -> x0, local copies, waits for them, and re-layouts: 16.3 us -> none
    pallas_call x1, Pallas kernels: 69.1 us -> 61.1 us  [run_main(): pl.pallas_call(main_kernel, out_shape=tuple((s((32, n, 16, 128), bf16) fo...]
    pallas_call x1, Pallas kernels: 2.17 us -> 3.76 us  [run_final(): pl.pallas_call(functools.partial(final_kernel, scale), out_shape=(s((196,...]
where the time goes in v3:
time: 65.8 us; the launch traced here: 65.7 us
  Pallas kernels  64.9 us (99%)
  between operations  0.8 us (1%)
    pallas_call x1, Pallas kernels, run_main(): pl.pallas_call(main_kernel, out_shape=tuple((s((32, n, 16, 128), bf16) fo...  61.1 us
    pallas_call x1, Pallas kernels, run_final(): pl.pallas_call(functools.partial(final_kernel, scale), out_shape=(s((196,...  3.76 us

profile of v3, /device:TPU:1, one launch (start us, length us, event | category | flops | bytes accessed | tf_op | source)
XLA Modules:
  0.0 65.7 jit_solution(16565357497915465291)
XLA Ops:
  0.6 61.1 %shard_map.233 = (bf16[32,3,16,128]{3,2,1,0:T(8,128)(2,1)}, bf16[32,3,16,128]{3,2,1,0:T(8,128)(2,1)}, bf16[32,4,16,128]{3,2,1,0:T(8,128)(2,1)}, bf16[392,384]{1,0:T(8,128)(2,1)}, bf16[192,384]{1,0:T(8,128)(2,1)}) custom-call(bf16[196,2,384]{2,1,0:T(2,128)(2,1)} %bitcast.13, bf16[196,2,384]{2,1,0:T(2,128)(2,1)} %bitcast.11, ...), custom_call_target="tpu_custom_call" | custom-call | tf_op jit(solution)/shard_map/pallas_call | solution.py:402
  61.8 3.8 %shard_map.234 = (bf16[196,2,384]{2,1,0:T(2,128)(2,1)}, f32[384]{0:T(512)}, f32[384]{0:T(512)}, f32[384,1152]{1,0:T(8,128)}, f32[1152]{0:T(1024)}, /*index=5*/f3...) custom-call(bf16[32,3,16,128]{3,2,1,0:T(8,128)(2,1)} %get-tuple-element.21.g0_in, ...), custom_call_target="tpu_custom_call" | custom-call | tf_op jit(solution)/shard_map/pallas_call | solution.py:461

commit v4 on v3

--- a/solution.py
+++ b/solution.py
@@ -74,11 +74,12 @@
 def main_kernel(
     x_in, u_in, ps_in, pw1_in, table_in, eb_in, ea_in, gain_in, shift_in, wqkv_in, bqkv_in, wproj_in, pw2_in, hm_in,
     q2_in, q1_in, er_in,
-    out0, out1, out2, gl, hout,
+    out0_o, out1_o, out2_o, gl_o, hout_o,
+    out0, out1, out2, gl, hout, store,
     x, u, ps, pw1, table, eb, ea, gain, shift, wqkv, bqkv, wproj, pw2, hm, q2, q1, er, load,
     flat, box, rx, xhat, rstd, norm, up, qkv, gat, attn, gq, tvar, gtab, tab, small, gsh,
     g, r0, s1, r1_0, r1_1, r1_2, acc, sg, t0, ts, t1, tacc, s2_0, s2_1, s2_2, hbox,
-    hs, hr, bs, br, p0s, p0r, p1s, p1r, q0s, q0r, q1s, q1r, p2s, p2r, p4s, p4r, p5s, p5r,
+    hs, hr, bs, br, p0s, p0r, p1s, p1r, q0s, q0r, q1s, q1r, p2s, p2r, p4s, p4r, p5s, p5r, p6s, p6r,
 ):
     px, py, z, core = place()
     me = px * 4 + py
@@ -231,7 +232,9 @@
     lax.fori_loop(0, 8 // UNROLL, windows, 0)
 
     out, r1, s2 = (out0, out1, out2), (r1_0, r1_1, r1_2), (s2_0, s2_1, s2_2)
-    order = list(range(1, 16)) + [0]
+    hops = lambda k: min(k // 4, 4 - k // 4) + min(k % 4, 4 - k % 4)
+    order = sorted(range(16), key=hops, reverse=True)
+    far = (4, 3, 5, 2, 6, 1, 7)
     c0, c1, c2, c4, c5, d1 = [], [], [], [], [], [None] * 16
 
     def chunk(k):
@@ -278,7 +281,7 @@
                 tacc[...] += t[:8] + t[8:]
             s2[seg][z, 3] = split(tacc[...])
         cs = []
-        for k in range(1, 8):
+        for k in far:
             c = send(s2[seg].at[z], s2[seg].at[z], p2s.at[seg, k], p2r.at[seg, k], depth(k))
             c.start()
             cs.append(c)
@@ -296,42 +299,46 @@
         out[seg][mine, 0:3] = a[0:3].astype(bf16)
         if seg == 2:
             out[seg][mine, 3] = split(a[3, :8] + a[3, 8:])
-        for k in range(1, 16):
+        for k in order[:15]:
             c = send(out[seg].at[mine], out[seg].at[mine], p4s.at[seg, k], p4r.at[seg, k], plane(k))
             c.start()
             c4.append(c)
 
     def hand_over(seg):
-        for k in range(1, 16):
+        if seg < 2:
+            for k in range(1, 16):
+                f = core * 16 + plane_from(k)
+                send(out[seg].at[f], out[seg].at[f], p4s.at[seg, k], p4r.at[seg, k], plane(k)).wait_recv()
+            half = pl.ds(core * 16, 16)
+            c = send(out[seg].at[half], out[seg].at[half], p5s.at[seg], p5r.at[seg], sib)
+            c.start()
+            c5.append(c)
+            return
+        for k in [0] + order[14::-1]:
             f = core * 16 + plane_from(k)
-            send(out[seg].at[f], out[seg].at[f], p4s.at[seg, k], p4r.at[seg, k], plane(k)).wait_recv()
-        half = pl.ds(core * 16, 16)
-        c = send(out[seg].at[half], out[seg].at[half], p5s.at[seg], p5r.at[seg], sib)
+            if k:
+                send(out[seg].at[f], out[seg].at[f], p4s.at[seg, k], p4r.at[seg, k], plane(k)).wait_recv()
+            c = send(out[seg].at[f], out[seg].at[f], p6s.at[k], p6r.at[k], sib)
+            c.start()
+            c5.append(c)
+
+    def keep(i, src, dst):
+        c = pltpu.make_async_copy(src, dst, store.at[i])
         c.start()
-        c5.append(c)
+        kept.append(c)
+
+    kept = []
+    spread(0)
 
     gn = dot(gq[...], wqkv[...], 1, 1).astype(bf16).astype(f32)
     xh = xhat[...]
+    spread(1)
+    spread(2)
     a = jnp.sum(gn * xh, axis=0, keepdims=True)
     b = jnp.sum(gn, axis=0, keepdims=True)
     for n in range(3):
         small[n : n + 1] = a[:, 128 * n : 128 * n + 128]
         small[3 + n : 4 + n] = b[:, 128 * n : 128 * n + 128]
-
-    for seg in range(3):
-        spread(seg)
-
-    gg = gn * gain[...].reshape(1, 384)
-    m1 = jnp.sum(gg, axis=1, keepdims=True) * (1.0 / 384)
-    m2 = jnp.sum(gg * xh, axis=1, keepdims=True) * (1.0 / 384)
-    gsh[...] = ((gg - m1 - xh * m2) * rstd[...]).astype(bf16)
-    hbox[...] = dot(q2[...], gsh[...]).astype(bf16)
-    back = []
-    for i, (d, (lo, n)) in enumerate(zip(((rp, z, scene), (row, zp, scene), (rp, zp, scene)), pieces)):
-        c = send(hbox.at[pl.ds(lo, n)], hout.at[pl.ds(lo, n)], bs.at[i], br.at[i], d)
-        c.start()
-        back.append(c)
-    gl[...] = dot(q1[...], gsh[...]).astype(bf16)
 
     ones = jnp.ones((16, 512), bf16)
     sq = dot(ones, gq[...])[0:1]
@@ -374,21 +381,43 @@
         else:
             tacc[...] = total
     deepen(1)
+    gg = gn * gain[...].reshape(1, 384)
+    m1 = jnp.sum(gg, axis=1, keepdims=True) * (1.0 / 384)
+    m2 = jnp.sum(gg * xh, axis=1, keepdims=True) * (1.0 / 384)
+    gsh[...] = ((gg - m1 - xh * m2) * rstd[...]).astype(bf16)
+    hbox[...] = dot(q2[...], gsh[...]).astype(bf16)
+    back = []
+    for i, (d, (lo, n)) in enumerate(zip(((rp, z, scene), (row, zp, scene), (rp, zp, scene)), pieces)):
+        c = send(hbox.at[pl.ds(lo, n)], hout.at[pl.ds(lo, n)], bs.at[i], br.at[i], d)
+        c.start()
+        back.append(c)
+    gl[...] = dot(q1[...], gsh[...]).astype(bf16)
+
+    keep(3, gl, gl_o)
     finish(0)
     deepen(2)
     finish(1)
     hand_over(0)
     finish(2)
     hand_over(1)
-    hand_over(2)
-    for seg in range(3):
-        other = pl.ds((1 - core) * 16, 16)
-        send(out[seg].at[other], out[seg].at[other], p5s.at[seg], p5r.at[seg], sib).wait_recv()
     for c in back:
         c.wait_recv()
+    keep(4, hout, hout_o)
+    half, other = pl.ds(core * 16, 16), pl.ds((1 - core) * 16, 16)
+    send(out0.at[half], out0.at[other], p5s.at[0], p5r.at[0], sib).wait_recv()
+    keep(0, out0, out0_o)
+    hand_over(2)
+    send(out1.at[half], out1.at[other], p5s.at[1], p5r.at[1], sib).wait_recv()
+    keep(1, out1, out1_o)
+    for k in [0] + order[14::-1]:
+        f = (1 - core) * 16 + plane_from(k)
+        send(out2.at[f], out2.at[f], p6s.at[k], p6r.at[k], sib).wait_recv()
+    keep(2, out2, out2_o)
     for c in halo + back + c0 + c1[0] + c1[1] + c1[2] + [d0] + d1 + c2[0] + c2[1] + c2[2] + c4 + c5:
         if c is not None:
             c.wait_send()
+    for c in kept:
+        c.wait()
 
 
 def run_main(x, u, gain, shift, wqkv, bqkv, wproj, table, maps):
@@ -396,15 +425,16 @@
     c = lambda a: jnp.asarray(a, bf16)
     S, s, D = pltpu.VMEM, jax.ShapeDtypeStruct, pltpu.SemaphoreType.DMA
     sems = [D((n,)) for n in (6, 6, 3, 3, 3, 3)] + [D((3, 16)), D((3, 16)), D(()), D(()), D((16,)), D((16,))]
-    sems += [D((3, 8)), D((3, 8)), D((3, 16)), D((3, 16)), D((3,)), D((3,))]
+    sems += [D((3, 8)), D((3, 8)), D((3, 16)), D((3, 16)), D((2,)), D((2,)), D((16,)), D((16,))]
     j = jnp.asarray
     args = (x, u, c(ps), c(pw1), table, j(eb), j(ea), gain, shift, wqkv, bqkv, wproj, c(pw2), c(hm), c(pw2.T), c(pw1.T), j(er))
+    outs = tuple(s((32, n, 16, 128), bf16) for n in (3, 3, 4)) + (s((392, 384), bf16), s((192, 384), bf16))
     return pl.pallas_call(
         main_kernel,
-        out_shape=tuple(s((32, n, 16, 128), bf16) for n in (3, 3, 4)) + (s((392, 384), bf16), s((192, 384), bf16)),
+        out_shape=outs,
         in_specs=[pl.BlockSpec(memory_space=pltpu.HBM)] * 17,
-        out_specs=(V,) * 5,
-        scratch_shapes=[S(a.shape, a.dtype) for a in args] + [D((17,))] + [
+        out_specs=(pl.BlockSpec(memory_space=pltpu.HBM),) * 5,
+        scratch_shapes=[S(o.shape, o.dtype) for o in outs] + [D((5,))] + [S(a.shape, a.dtype) for a in args] + [D((17,))] + [
             S((392, 768), bf16), S((2, 192, 384), bf16), S((2, 192, 384), bf16),
             S((512, 384), f32), S((512, 1), f32), S((512, 384), bf16), S((512, 384), bf16),
             S((512, 1152), bf16), S((512, 384), bf16), S((512, 384), bf16), S((512, 1152), bf16),
@@ -420,24 +450,38 @@
 
 def final_kernel(
     scale, g0_in, g1_in, g2_in, u_in, gl_in, hr_in, q3_in,
-    gx_out, a_out, b_out, wq_out, bq_out, wp_out, bp_out, t_out,
-    g0, g1, g2, u, gl, hr, q3, load, small, tab,
+    gx_o, wq_o, wp_o, a_out, b_out, bq_out, bp_out, t_out,
+    g0, g1, g2, u, gl, hr, q3, load, gx, wq, wp, store, small, tab,
 ):
-    pairs = ((g0_in, g0), (g1_in, g1), (g2_in, g2), (u_in, u), (gl_in, gl), (hr_in, hr), (q3_in, q3))
+    pairs = ((g0_in, g0), (g1_in, g1), (g2_in, g2), (hr_in, hr), (q3_in, q3), (gl_in, gl), (u_in, u))
     loads = [pltpu.make_async_copy(a, b, load.at[i]) for i, (a, b) in enumerate(pairs)]
     for c in loads:
         c.start()
-    for c in loads:
+    stores = []
+
+    def put(src, dst):
+        c = pltpu.make_async_copy(src, dst, store.at[len(stores)])
+        c.start()
+        stores.append(c)
+
+    for seg, g in enumerate((g0, g1, g2)):
+        loads[seg].wait()
+        for n in range(4):
+            lb = 4 * seg + n
+            dst, l = (wp, lb) if lb < 3 else (wq, lb - 3)
+            for i in range(24):
+                t = n * 24 + i
+                dst[16 * i : 16 * i + 16, 128 * l : 128 * l + 128] = g[t // 3, t % 3].astype(f32) * scale
+        lanes = (pl.ds(0, 128), pl.ds(128, 512), pl.ds(640, 512))[seg]
+        put(wq.at[:, lanes], wq_o.at[:, lanes])
+        if seg == 0:
+            put(wp, wp_o)
+    for c in loads[3:]:
         c.wait()
     got = gl[...].astype(f32) + dot(q3[...], hr[...])
     for p in range(196):
-        gx_out[p] = (u[p].astype(f32) + got[2 * p : 2 * p + 2]).astype(bf16)
-    for lb in range(12):
-        dst, l = (wp_out, lb) if lb < 3 else (wq_out, lb - 3)
-        g = (g0, g1, g2)[lb // 4]
-        for i in range(24):
-            t = (lb % 4) * 24 + i
-            dst[16 * i : 16 * i + 16, 128 * l : 128 * l + 128] = g[t // 3, t % 3].astype(f32) * scale
+        gx[p] = (u[p].astype(f32) + got[2 * p : 2 * p + 2]).astype(bf16)
+    put(gx, gx_o)
     for c in range(6):
         t = g2[c, 3].astype(f32)
         small[8 * c : 8 * c + 8] = (t[:8] + t[8:]) * scale
@@ -453,21 +497,24 @@
         tab[h : h + 1, 0:128] = small[18 + 2 * h : 19 + 2 * h]
         tab[h : h + 1, 128:256] = small[19 + 2 * h : 20 + 2 * h]
     t_out[...] = tab[0:12, 0:169]
+    for c in stores:
+        c.wait()
 
 
 def run_final(scale, g0, g1, g2, u, gl, hr, maps):
     s = jax.ShapeDtypeStruct
     args = (g0, g1, g2, u, gl, hr, jnp.asarray(maps[2].T, bf16))
+    big = (s((196, 2, 384), bf16), s((384, 1152), f32), s((384, 384), f32))
     return pl.pallas_call(
         functools.partial(final_kernel, scale),
-        out_shape=(
-            s((196, 2, 384), bf16), s((384,), f32), s((384,), f32), s((384, 1152), f32),
-            s((1152,), f32), s((384, 384), f32), s((384,), f32), s((12, 169), f32),
-        ),
+        out_shape=big
+        + (s((384,), f32), s((384,), f32), s((1152,), f32), s((384,), f32), s((12, 169), f32)),
         in_specs=[pl.BlockSpec(memory_space=pltpu.HBM)] * 7,
-        out_specs=(V,) * 8,
+        out_specs=(pl.BlockSpec(memory_space=pltpu.HBM),) * 3 + (V,) * 5,
         scratch_shapes=[pltpu.VMEM(a.shape, a.dtype) for a in args]
-        + [pltpu.SemaphoreType.DMA((7,)), pltpu.VMEM((48, 128), f32), pltpu.VMEM((16, 256), f32)],
+        + [pltpu.SemaphoreType.DMA((7,))]
+        + [pltpu.VMEM(a.shape, a.dtype) for a in big]
+        + [pltpu.SemaphoreType.DMA((5,)), pltpu.VMEM((48, 128), f32), pltpu.VMEM((16, 256), f32)],
         compiler_params=pltpu.CompilerParams(vmem_limit_bytes=62 << 20),
     )(*args)
 
@@ -478,7 +525,7 @@
     u = grad_out.transpose(1, 2, 0, 3).reshape(196, 2, 384)
     g0, g1, g2, gl, hr = run_main(x, u, norm_gain, norm_shift, qkv_weight, qkv_bias, proj_weight, bias_table.T, maps)
     scale = 1.0 / math.sqrt(8 * 112 * 112)
-    gx, a, b, wq, bq, wp, bp, t = run_final(scale, g0, g1, g2, u, gl, hr, maps)
+    gx, wq, wp, a, b, bq, bp, t = run_final(scale, g0, g1, g2, u, gl, hr, maps)
     return gx.reshape(14, 14, 2, 384).transpose(2, 0, 1, 3), a, b, wq, bq, wp, bp, t.T
 
 

time: 65.8 us -> 62.7 us (0.953)
  Pallas kernels: 64.9 us -> 61.8 us
    pallas_call x2, Pallas kernels: 64.9 us -> 61.8 us  [the longest x1 58.2 us: run_main(): pl.pallas_call(main_kernel, out_shape=outs, in_specs=[pl.BlockSpec(memory...]
where the time goes in v4:
time: 62.7 us; the launch traced here: 62.6 us
  Pallas kernels  61.8 us (99%)
  between operations  0.8 us (1%)
    pallas_call x1, Pallas kernels, run_main(): pl.pallas_call(main_kernel, out_shape=outs, in_specs=[pl.BlockSpec(memory...  58.2 us
    pallas_call x1, Pallas kernels, run_final(): pl.pallas_call(functools.partial(final_kernel, scale), out_shape=big + (s...  3.54 us

profile of v4, /device:TPU:1, one launch (start us, length us, event | category | flops | bytes accessed | tf_op | source)
XLA Modules:
  0.0 62.6 jit_solution(851745693214059291)
XLA Ops:
  0.6 58.2 %shard_map.233 = (bf16[32,3,16,128]{3,2,1,0:T(8,128)(2,1)}, bf16[32,3,16,128]{3,2,1,0:T(8,128)(2,1)}, bf16[32,4,16,128]{3,2,1,0:T(8,128)(2,1)}, bf16[392,384]{1,0:T(8,128)(2,1)}, bf16[192,384]{1,0:T(8,128)(2,1)}) custom-call(bf16[196,2,384]{2,1,0:T(2,128)(2,1)} %bitcast.13, bf16[196,2,384]{2,1,0:T(2,128)(2,1)} %bitcast.11, ...), custom_call_target="tpu_custom_call" | custom-call | tf_op jit(solution)/shard_map/pallas_call | solution.py:432
  58.9 3.5 %shard_map.234 = (bf16[196,2,384]{2,1,0:T(2,128)(2,1)}, f32[384,1152]{1,0:T(8,128)}, f32[384,384]{1,0:T(8,128)}, f32[384]{0:T(512)}, f32[384]{0:T(512)}, /*index...) custom-call(bf16[32,3,16,128]{3,2,1,0:T(8,128)(2,1)} %get-tuple-element.21.g0_in, ...), custom_call_target="tpu_custom_call" | custom-call | tf_op jit(solution)/shard_map/pallas_call | solution.py:508

commit v5 on v4

--- a/solution.py
+++ b/solution.py
@@ -11,7 +11,7 @@
 
 WIN, SHIFT, NORM_EPS, MASKED = 7, 3, 1e-05, -1e30
 LOG2E = 1.4426950408889634
-UNROLL = 4
+UNROLL = 8
 HIGH = lax.Precision.HIGHEST
 MESH = pl.DeviceIdType.MESH
 f32, bf16 = jnp.float32, jnp.bfloat16
@@ -79,7 +79,7 @@
     x, u, ps, pw1, table, eb, ea, gain, shift, wqkv, bqkv, wproj, pw2, hm, q2, q1, er, load,
     flat, box, rx, xhat, rstd, norm, up, qkv, gat, attn, gq, tvar, gtab, tab, small, gsh,
     g, r0, s1, r1_0, r1_1, r1_2, acc, sg, t0, ts, t1, tacc, s2_0, s2_1, s2_2, hbox,
-    hs, hr, bs, br, p0s, p0r, p1s, p1r, q0s, q0r, q1s, q1r, p2s, p2r, p4s, p4r, p5s, p5r, p6s, p6r,
+    hs, hr, bs, br, p0s, p0r, p1s, p1r, q0s, q0r, q1s, q1r, p2s, p2r, p4s, p4r, p5s, p5r,
 ):
     px, py, z, core = place()
     me = px * 4 + py
@@ -90,9 +90,6 @@
 
     def plane(k):
         return at(lax.rem(px + k // 4, 4), lax.rem(py + k % 4, 4), z, core)
-
-    def plane_from(k):
-        return lax.rem(px + 4 - k // 4, 4) * 4 + lax.rem(py + 4 - k % 4, 4)
 
     def depth(k):
         return at(px, py, lax.rem(z + k, 8), core)
@@ -235,7 +232,10 @@
     hops = lambda k: min(k // 4, 4 - k // 4) + min(k % 4, 4 - k % 4)
     order = sorted(range(16), key=hops, reverse=True)
     far = (4, 3, 5, 2, 6, 1, 7)
-    c0, c1, c2, c4, c5, d1 = [], [], [], [], [], [None] * 16
+    c0, c5 = [], []
+
+    def all_of(what, sem):
+        pltpu.make_async_copy(what, what, sem).wait()
 
     def chunk(k):
         return lax.rem(px + k // 4, 4) * 4 + lax.rem(py + k % 4, 4)
@@ -256,43 +256,36 @@
 
     def spread(seg):
         c0[seg].wait_recv()
-        cs = [None] * 16
         for k in order:
             c = chunk(k)
             total = g[seg, core * 16 + c].astype(f32) + r0[seg, c].astype(f32)
             if k:
                 s1[seg, c] = total.astype(bf16)
-                cs[k] = send(s1.at[seg, c], r1[seg].at[k], p1s.at[seg, k], p1r.at[seg, k], plane(k))
-                cs[k].start()
+                c = send(s1.at[seg, c], r1[seg].at[k], p1s.at[seg], p1r.at[seg], plane(k))
+                c.start()
             else:
                 acc[seg] = total
-        c1.append(cs)
 
     def deepen(seg):
         a = acc[seg]
+        all_of(r1[seg].at[pl.ds(1, 15)], p1r.at[seg])
         for k in range(1, 16):
-            c1[seg][k].wait_recv()
             a = a + r1[seg][k].astype(f32)
         s2[seg][z, 0:3] = a.astype(bf16)
         if seg == 2:
+            all_of(t1.at[pl.ds(1, 15)], q1r)
             for k in range(1, 16):
-                d1[k].wait_recv()
                 t = t1[k].astype(f32)
                 tacc[...] += t[:8] + t[8:]
             s2[seg][z, 3] = split(tacc[...])
-        cs = []
         for k in far:
-            c = send(s2[seg].at[z], s2[seg].at[z], p2s.at[seg, k], p2r.at[seg, k], depth(k))
+            c = send(s2[seg].at[z], s2[seg].at[z], p2s.at[seg], p2r.at[seg], depth(k))
             c.start()
-            cs.append(c)
-        c2.append(cs)
 
     mine = core * 16 + me
 
     def finish(seg):
-        for k in range(1, 8):
-            fr = lax.rem(z + 8 - k, 8)
-            send(s2[seg].at[fr], s2[seg].at[fr], p2s.at[seg, k], p2r.at[seg, k], depth(k)).wait_recv()
+        all_of(s2[seg].at[pl.ds(0, 7)], p2r.at[seg])
         a = s2[seg][0].astype(f32)
         for t in range(1, 8):
             a = a + s2[seg][t].astype(f32)
@@ -300,27 +293,15 @@
         if seg == 2:
             out[seg][mine, 3] = split(a[3, :8] + a[3, 8:])
         for k in order[:15]:
-            c = send(out[seg].at[mine], out[seg].at[mine], p4s.at[seg, k], p4r.at[seg, k], plane(k))
+            c = send(out[seg].at[mine], out[seg].at[mine], p4s.at[seg], p4r.at[seg], plane(k))
             c.start()
-            c4.append(c)
 
     def hand_over(seg):
-        if seg < 2:
-            for k in range(1, 16):
-                f = core * 16 + plane_from(k)
-                send(out[seg].at[f], out[seg].at[f], p4s.at[seg, k], p4r.at[seg, k], plane(k)).wait_recv()
-            half = pl.ds(core * 16, 16)
-            c = send(out[seg].at[half], out[seg].at[half], p5s.at[seg], p5r.at[seg], sib)
-            c.start()
-            c5.append(c)
-            return
-        for k in [0] + order[14::-1]:
-            f = core * 16 + plane_from(k)
-            if k:
-                send(out[seg].at[f], out[seg].at[f], p4s.at[seg, k], p4r.at[seg, k], plane(k)).wait_recv()
-            c = send(out[seg].at[f], out[seg].at[f], p6s.at[k], p6r.at[k], sib)
-            c.start()
-            c5.append(c)
+        all_of(out[seg].at[pl.ds(0, 15)], p4r.at[seg])
+        half = pl.ds(core * 16, 16)
+        c = send(out[seg].at[half], out[seg].at[half], p5s.at[seg], p5r.at[seg], sib)
+        c.start()
+        c5.append(c)
 
     def keep(i, src, dst):
         c = pltpu.make_async_copy(src, dst, store.at[i])
@@ -376,8 +357,8 @@
         total = total[:8] + total[8:]
         if k:
             ts[c] = split(total)
-            d1[k] = send(ts.at[c], t1.at[k], q1s.at[k], q1r.at[k], plane(k))
-            d1[k].start()
+            c = send(ts.at[c], t1.at[k], q1s, q1r, plane(k))
+            c.start()
         else:
             tacc[...] = total
     deepen(1)
@@ -409,13 +390,15 @@
     hand_over(2)
     send(out1.at[half], out1.at[other], p5s.at[1], p5r.at[1], sib).wait_recv()
     keep(1, out1, out1_o)
-    for k in [0] + order[14::-1]:
-        f = (1 - core) * 16 + plane_from(k)
-        send(out2.at[f], out2.at[f], p6s.at[k], p6r.at[k], sib).wait_recv()
+    send(out2.at[half], out2.at[other], p5s.at[2], p5r.at[2], sib).wait_recv()
     keep(2, out2, out2_o)
-    for c in halo + back + c0 + c1[0] + c1[1] + c1[2] + [d0] + d1 + c2[0] + c2[1] + c2[2] + c4 + c5:
-        if c is not None:
-            c.wait_send()
+    for c in halo + back + c0 + [d0] + c5:
+        c.wait_send()
+    for seg in range(3):
+        all_of(r1[seg].at[pl.ds(1, 15)], p1s.at[seg])
+        all_of(s2[seg].at[pl.ds(0, 7)], p2s.at[seg])
+        all_of(out[seg].at[pl.ds(0, 15)], p4s.at[seg])
+    all_of(t1.at[pl.ds(1, 15)], q1s)
     for c in kept:
         c.wait()
 
@@ -424,8 +407,7 @@
     pw1, pw2, ps, ea, eb, er, hm = maps
     c = lambda a: jnp.asarray(a, bf16)
     S, s, D = pltpu.VMEM, jax.ShapeDtypeStruct, pltpu.SemaphoreType.DMA
-    sems = [D((n,)) for n in (6, 6, 3, 3, 3, 3)] + [D((3, 16)), D((3, 16)), D(()), D(()), D((16,)), D((16,))]
-    sems += [D((3, 8)), D((3, 8)), D((3, 16)), D((3, 16)), D((2,)), D((2,)), D((16,)), D((16,))]
+    sems = [D((n,)) for n in (6, 6, 3, 3, 3, 3, 3, 3)] + [D(())] * 4 + [D((3,))] * 6
     j = jnp.asarray
     args = (x, u, c(ps), c(pw1), table, j(eb), j(ea), gain, shift, wqkv, bqkv, wproj, c(pw2), c(hm), c(pw2.T), c(pw1.T), j(er))
     outs = tuple(s((32, n, 16, 128), bf16) for n in (3, 3, 4)) + (s((392, 384), bf16), s((192, 384), bf16))

time: 62.7 us -> 59.5 us (0.949)
  Pallas kernels: 61.8 us -> 58.6 us
    pallas_call x1, Pallas kernels: 58.2 us -> 55 us  [run_main(): pl.pallas_call(main_kernel, out_shape=outs, in_specs=[pl.BlockSpec(memory...]
where the time goes in v5:
time: 59.5 us; the launch traced here: 59.4 us
  Pallas kernels  58.6 us (98%)
  between operations  0.8 us (1%)
    pallas_call x1, Pallas kernels, run_main(): pl.pallas_call(main_kernel, out_shape=outs, in_specs=[pl.BlockSpec(memory...  55 us
    pallas_call x1, Pallas kernels, run_final(): pl.pallas_call(functools.partial(final_kernel, scale), out_shape=big + (s...  3.53 us

profile of v5, /device:TPU:1, one launch (start us, length us, event | category | flops | bytes accessed | tf_op | source)
XLA Modules:
  0.0 59.4 jit_solution(11257152900661811825)
XLA Ops:
  0.6 55.0 %shard_map.233 = (bf16[32,3,16,128]{3,2,1,0:T(8,128)(2,1)}, bf16[32,3,16,128]{3,2,1,0:T(8,128)(2,1)}, bf16[32,4,16,128]{3,2,1,0:T(8,128)(2,1)}, bf16[392,384]{1,0:T(8,128)(2,1)}, bf16[192,384]{1,0:T(8,128)(2,1)}) custom-call(bf16[196,2,384]{2,1,0:T(2,128)(2,1)} %bitcast.13, bf16[196,2,384]{2,1,0:T(2,128)(2,1)} %bitcast.11, ...), custom_call_target="tpu_custom_call" | custom-call | tf_op jit(solution)/shard_map/pallas_call | solution.py:414
  55.7 3.5 %shard_map.234 = (bf16[196,2,384]{2,1,0:T(2,128)(2,1)}, f32[384,1152]{1,0:T(8,128)}, f32[384,384]{1,0:T(8,128)}, f32[384]{0:T(512)}, f32[384]{0:T(512)}, /*index...) custom-call(bf16[32,3,16,128]{3,2,1,0:T(8,128)(2,1)} %get-tuple-element.21.g0_in, ...), custom_call_target="tpu_custom_call" | custom-call | tf_op jit(solution)/shard_map/pallas_call | solution.py:490

commit v6 on v5

--- a/solution.py
+++ b/solution.py
@@ -378,8 +378,8 @@
     finish(0)
     deepen(2)
     finish(1)
+    finish(2)
     hand_over(0)
-    finish(2)
     hand_over(1)
     for c in back:
         c.wait_recv()

time: 59.5 us -> 59.3 us (level)
  no operation moved by 1% of the time
where the time goes in v6:
time: 59.3 us; the launch traced here: 59.2 us
  Pallas kernels  58.4 us (98%)
  between operations  0.8 us (1%)
    pallas_call x1, Pallas kernels, run_main(): pl.pallas_call(main_kernel, out_shape=outs, in_specs=[pl.BlockSpec(memory...  54.9 us
    pallas_call x1, Pallas kernels, run_final(): pl.pallas_call(functools.partial(final_kernel, scale), out_shape=big + (s...  3.53 us

profile of v6, /device:TPU:1, one launch (start us, length us, event | category | flops | bytes accessed | tf_op | source)
XLA Modules:
  0.0 59.2 jit_solution(6122668532210097419)
XLA Ops:
  0.6 54.9 %shard_map.233 = (bf16[32,3,16,128]{3,2,1,0:T(8,128)(2,1)}, bf16[32,3,16,128]{3,2,1,0:T(8,128)(2,1)}, bf16[32,4,16,128]{3,2,1,0:T(8,128)(2,1)}, bf16[392,384]{1,0:T(8,128)(2,1)}, bf16[192,384]{1,0:T(8,128)(2,1)}) custom-call(bf16[196,2,384]{2,1,0:T(2,128)(2,1)} %bitcast.13, bf16[196,2,384]{2,1,0:T(2,128)(2,1)} %bitcast.11, ...), custom_call_target="tpu_custom_call" | custom-call | tf_op jit(solution)/shard_map/pallas_call | solution.py:414
  55.5 3.5 %shard_map.234 = (bf16[196,2,384]{2,1,0:T(2,128)(2,1)}, f32[384,1152]{1,0:T(8,128)}, f32[384,384]{1,0:T(8,128)}, f32[384]{0:T(512)}, f32[384]{0:T(512)}, /*index...) custom-call(bf16[32,3,16,128]{3,2,1,0:T(8,128)(2,1)} %get-tuple-element.21.g0_in, ...), custom_call_target="tpu_custom_call" | custom-call | tf_op jit(solution)/shard_map/pallas_call | solution.py:490
